TPU v7x, 32 devices: a whole 2x2x4 slice. The times are simulated.
32 devices in a mesh: dp: 8 (over z, x), mp: 4 (over y, core).
Axes of the slice: x: 2, y: 2, z: 4, core: 2. Of those that a mesh axis runs over, the one named last changes fastest.
Arguments:
- tokens: bfloat16 [8, 2048, 1024], P('dp'), may hold values from -6 to 6
- doc_lengths: int32 [8, 8], P('dp'), may hold values from 1 to 1024, 2048 in all within a row
- cotangent: bfloat16 [8, 2048, 1024], P('dp'), may hold values from -6 to 6
- norm_gain: bfloat16 [1024], P('dp'), may hold values from 0.5 to 1.5
- w_query: bfloat16 [1024, 1024], P('dp', 'mp'), may hold values from -0.1875 to 0.1875
- w_key: bfloat16 [1024, 1024], P('dp', 'mp'), may hold values from -0.1875 to 0.1875
- w_value: bfloat16 [1024, 1024], P('dp', 'mp'), may hold values from -0.1875 to 0.1875
- w_beta: bfloat16 [1024, 8], P('dp', 'mp'), may hold values from -0.1875 to 0.1875
- conv_taps: bfloat16 [8, 12, 128], P('mp', None, 'dp'), may hold values from -3 to 3
- head_gain: bfloat16 [128], P('dp'), may hold values from 0.5 to 1.5
- w_out: bfloat16 [1024, 1024], P('mp', 'dp'), may hold values from -0.1875 to 0.1875
- mlp_gain: bfloat16 [1024], P('dp'), may hold values from 0.5 to 1.5
- w_gate: bfloat16 [1024, 2816], P('dp', 'mp'), may hold values from -0.1875 to 0.1875
- w_up: bfloat16 [1024, 2816], P('dp', 'mp'), may hold values from -0.1875 to 0.1875
- w_down: bfloat16 [2816, 1024], P('mp', 'dp'), may hold values from -0.109375 to 0.109375
Outputs:
- layer_out: bfloat16 [8, 2048, 1024], P('dp')
- token_grad: float32 [8, 2048, 1024], P('dp')
- grad_norm_gain: float32 [1024], P('dp')
- grad_w_query: float32 [1024, 1024], P('dp', 'mp')
- grad_w_key: float32 [1024, 1024], P('dp', 'mp')
- grad_w_value: float32 [1024, 1024], P('dp', 'mp')
- grad_w_beta: float32 [1024, 8], P('dp', 'mp')
- grad_conv_taps: float32 [8, 12, 128], P('mp', None, 'dp')
- grad_head_gain: float32 [128], P('dp')
- grad_w_out: float32 [1024, 1024], P('mp', 'dp')
- grad_mlp_gain: float32 [1024], P('dp')
- grad_w_gate: float32 [1024, 2816], P('dp', 'mp')
- grad_w_up: float32 [1024, 2816], P('dp', 'mp')
- grad_w_down: float32 [2816, 1024], P('mp', 'dp')
Inputs may be any that keep to these rules, and one draw needn't show every extreme that they name: `doc_lengths`: each row's 8 lengths sum to 2048, and in every row one of them is exactly 1024.
All inputs are finite; a program needn't handle non-finite values.
Results may differ from a plain program's by a relative error of at most 0.02.
Values may be sent and summed in bfloat16 or wider, within the bound.
No kernel may reach another device: no remote copies, remote signals or barrier semaphores. Data moves between devices by JAX's collectives and lax.ppermute only.
A program may use at most 320 MiB of HBM per device.

v0:
```python
import jax
import jax.numpy as jnp
from jax import lax
from jax.sharding import PartitionSpec as P

GROUP = 64


epsilon = 1e-06
highest_precision = lax.Precision.HIGHEST


def rms_norm(values, gain):
    return values * lax.rsqrt(jnp.mean(values * values, axis=-1, keepdims=True) + epsilon) * gain


def doc_layout(lengths, length):
    places = jnp.arange(length, dtype=jnp.int32)
    doc_ends = jnp.cumsum(lengths)
    passed = places[:, None] >= doc_ends[None, :]
    doc_ids = jnp.sum(passed.astype(jnp.int32), axis=1)
    starts = jnp.max(jnp.where(passed, doc_ends[None, :], 0), axis=1)
    return (doc_ids, places - starts)


def short_conv(inputs, kernel, offsets):
    reach_len = kernel.shape[0]
    summed = inputs * kernel[reach_len - 1]
    for behind in range(1, reach_len):
        shifted = jnp.pad(inputs, ((behind, 0), (0, 0)))[: inputs.shape[0]]
        usable = (offsets >= behind).astype(jnp.float32)[:, None]
        summed = summed + shifted * kernel[reach_len - 1 - behind] * usable
    return summed


def mixer_inputs(query_proj, key_proj, value_proj, beta_logit, conv_taps, offsets):
    head_count, kernel_rows, head_dim = conv_taps.shape
    reach_len = kernel_rows // 3
    length = query_proj.shape[0]

    def branch(inputs, branch_id):
        kernel = conv_taps[:, branch_id * reach_len : (branch_id + 1) * reach_len, :]
        kernel = kernel.transpose(1, 0, 2).reshape(reach_len, head_count * head_dim)
        return jax.nn.silu(short_conv(inputs, kernel, offsets)).reshape(
            length, head_count, head_dim
        )

    query_conv = branch(query_proj, 0)
    query_matrix = (
        query_conv
        * lax.rsqrt(jnp.sum(query_conv * query_conv, axis=-1, keepdims=True) + epsilon)
        * head_dim ** (-0.5)
    )
    key_conv = branch(key_proj, 1)
    incoming_keys = key_conv * lax.rsqrt(
        jnp.sum(key_conv * key_conv, axis=-1, keepdims=True) + epsilon
    )
    values_in = branch(value_proj, 2)
    return (query_matrix, incoming_keys, values_in, jax.nn.sigmoid(beta_logit))


def block_prepare(query_block, key_block, value_block, beta_block, ids_block):
    block_size = query_block.shape[1]
    order_idx = jnp.arange(block_size)
    same_doc = (ids_block[:, :, None] == ids_block[:, None, :]).astype(jnp.float32)
    strict_low = (order_idx[:, None] > order_idx[None, :]).astype(jnp.float32)
    incl_low = (order_idx[:, None] >= order_idx[None, :]).astype(jnp.float32)
    key_gram = jnp.einsum("nihd,njhd->nhij", key_block, key_block, precision=highest_precision)
    beta_heads = beta_block.transpose(0, 2, 1)
    lower_part = (
        (strict_low[None, :, :] * same_doc)[:, None, :, :] * beta_heads[:, :, :, None] * key_gram
    )
    identity = jnp.eye(block_size, dtype=jnp.float32)
    inverse = identity - lower_part
    power = lower_part
    span = 2
    while span < block_size:
        power = jnp.einsum("nhij,nhjk->nhik", power, power, precision=highest_precision)
        inverse = inverse + jnp.einsum(
            "nhij,nhjk->nhik", inverse, power, precision=highest_precision
        )
        span = span * 2
    scaled_both = (
        beta_block[:, :, :, None] * jnp.concatenate([key_block, value_block], axis=3)
    ).transpose(0, 2, 1, 3)
    solved = jnp.einsum("nhij,nhjd->nhid", inverse, scaled_both, precision=highest_precision)
    scores = (
        jnp.einsum("nihd,njhd->nhij", query_block, key_block, precision=highest_precision)
        * (incl_low[None, :, :] * same_doc)[:, None, :, :]
    )
    return (solved, scores, same_doc[:, :, block_size - 1])


def group_step(running_state_value, blocks):
    query_matrix, incoming_keys, solved, scores, last_doc, carried_state = blocks
    block_size = query_matrix.shape[0]
    head_dim = query_matrix.shape[2]
    decay_weight_block = solved[:, :, :head_dim]
    update_block = solved[:, :, head_dim:]
    fresh_value_rows = update_block - carried_state[None, :, None] * jnp.einsum(
        "noj,njb->nob", decay_weight_block, running_state_value, precision=highest_precision
    )
    state_for_query = jnp.einsum(
        "zmu,muj->mzj", query_matrix, running_state_value, precision=highest_precision
    )
    outputs = carried_state[None, :, None] * state_for_query + jnp.einsum(
        "hij,hjv->hiv", scores, fresh_value_rows, precision=highest_precision
    )
    updated_state = carried_state[block_size - 1] * running_state_value + jnp.einsum(
        "sbf,bsx->bfx",
        incoming_keys * last_doc[:, None, None],
        fresh_value_rows,
        precision=highest_precision,
    )
    return (updated_state, outputs.transpose(1, 0, 2))


def delta_rule(query_matrix, incoming_keys, values_in, beta_rows, doc_ids, offsets):
    length, head_count, head_dim = query_matrix.shape
    blocks_n = length // GROUP
    order_idx = jnp.arange(length, dtype=jnp.int32) % GROUP
    carried_state = (offsets > order_idx).astype(jnp.float32)

    def to_blocks(array_in):
        return array_in.reshape((blocks_n, GROUP) + array_in.shape[1:])

    query_blocks = to_blocks(query_matrix)
    key_blocks = to_blocks(incoming_keys)
    solved, scores, last_doc = block_prepare(
        query_blocks, key_blocks, to_blocks(values_in), to_blocks(beta_rows), to_blocks(doc_ids)
    )
    start_state = jnp.zeros((head_count, head_dim, head_dim), jnp.float32)
    final_state, outputs = lax.scan(
        jax.checkpoint(group_step),
        start_state,
        (query_blocks, key_blocks, solved, scores, last_doc, to_blocks(carried_state)),
    )
    return outputs.reshape(length, head_count, head_dim)


def rounded(values):
    return lax.optimization_barrier(values.astype(jnp.bfloat16)).astype(jnp.float32)


def matmul(left, right):
    return jnp.dot(left, right, preferred_element_type=jnp.float32)


def matmul_bt(left, right):
    return lax.dot_general(
        left, right, (((1,), (1,)), ((), ())), preferred_element_type=jnp.float32
    )


def matmul_at(left, right):
    return lax.dot_general(
        left, right, (((0,), (0,)), ((), ())), preferred_element_type=jnp.float32
    )


def on_device(
    tokens,
    doc_lengths,
    cotangent,
    norm_gain,
    w_query,
    w_key,
    w_value,
    w_beta,
    conv_taps,
    head_gain,
    w_out,
    mlp_gain,
    w_gate,
    w_up,
    w_down,
):
    seq_rows, length, width = tokens.shape
    row_total = seq_rows * length
    gain_one, query_all, key_all, value_all, beta_all, taps_all, head_all, out_all = (
        lax.all_gather(norm_gain, "dp", axis=0, tiled=True),
        lax.all_gather(w_query, "dp", axis=0, tiled=True),
        lax.all_gather(w_key, "dp", axis=0, tiled=True),
        lax.all_gather(w_value, "dp", axis=0, tiled=True),
        lax.all_gather(w_beta, "dp", axis=0, tiled=True),
        lax.all_gather(conv_taps, "dp", axis=2, tiled=True),
        lax.all_gather(head_gain, "dp", axis=0, tiled=True),
        lax.all_gather(w_out, "dp", axis=1, tiled=True),
    )
    flat_in = tokens.reshape(row_total, width).astype(jnp.float32)
    gain_one_f = gain_one.astype(jnp.float32)
    normed = rms_norm(flat_in, gain_one_f).astype(jnp.bfloat16)
    query_proj = matmul(normed, query_all)
    key_proj = matmul(normed, key_all)
    value_proj = matmul(normed, value_all)
    beta_logit = matmul(normed, beta_all)
    doc_ids, offsets = jax.vmap(lambda row_lengths: doc_layout(row_lengths, length))(doc_lengths)

    def rows_of(values):
        return values.reshape((seq_rows, length) + values.shape[1:])

    mix_rows = jax.vmap(mixer_inputs, in_axes=(0, 0, 0, 0, None, 0))
    mixed_in, mix_pull = jax.vjp(
        lambda q_rows, k_rows, v_rows, b_rows, t_taps: mix_rows(
            q_rows, k_rows, v_rows, b_rows, t_taps, offsets
        ),
        rows_of(query_proj),
        rows_of(key_proj),
        rows_of(value_proj),
        rows_of(beta_logit),
        taps_all.astype(jnp.float32),
    )
    query_matrix, incoming_keys, values_in, beta_rows = mixed_in
    core_rows = jax.vmap(delta_rule)
    core_out, core_pull = jax.vjp(
        lambda q_rows, k_rows, v_rows, b_rows: core_rows(
            q_rows, k_rows, v_rows, b_rows, doc_ids, offsets
        ),
        rounded(query_matrix),
        rounded(incoming_keys),
        rounded(values_in),
        beta_rows,
    )
    head_gain_f = head_all.astype(jnp.float32)
    head_normed = rms_norm(core_out, head_gain_f).astype(jnp.bfloat16).reshape(row_total, -1)
    mixer_part = matmul(head_normed, out_all)
    res_rows = flat_in + lax.psum(mixer_part, "mp")
    gain_two, gate_all, up_all, down_all = (
        lax.all_gather(mlp_gain, "dp", axis=0, tiled=True),
        lax.all_gather(w_gate, "dp", axis=0, tiled=True),
        lax.all_gather(w_up, "dp", axis=0, tiled=True),
        lax.all_gather(w_down, "dp", axis=1, tiled=True),
    )
    gain_two_f = gain_two.astype(jnp.float32)
    normed_part = rms_norm(res_rows, gain_two_f).astype(jnp.bfloat16)
    gate_vals = matmul(normed_part, gate_all)
    up_vals = matmul(normed_part, up_all)
    activated = (jax.nn.silu(gate_vals) * up_vals).astype(jnp.bfloat16)
    down_part = matmul(activated, down_all)
    layer_out = (
        res_rows + lax.psum(down_part.astype(jnp.bfloat16), "mp").astype(jnp.float32)
    ).astype(jnp.bfloat16)
    cot_low = cotangent.reshape(row_total, width)
    cot_flat = cot_low.astype(jnp.float32)
    gain_two, gate_all, up_all, down_all = (
        lax.all_gather(mlp_gain, "dp", axis=0, tiled=True),
        lax.all_gather(w_gate, "dp", axis=0, tiled=True),
        lax.all_gather(w_up, "dp", axis=0, tiled=True),
        lax.all_gather(w_down, "dp", axis=1, tiled=True),
    )
    gain_two_f = gain_two.astype(jnp.float32)
    d_hidden = matmul_bt(cot_low, down_all)
    sig_gate = jax.nn.sigmoid(gate_vals)
    d_gate = (d_hidden * up_vals * sig_gate * (1.0 + gate_vals * (1.0 - sig_gate))).astype(
        jnp.bfloat16
    )
    d_up = (d_hidden * gate_vals * sig_gate).astype(jnp.bfloat16)
    grad_down = matmul_at(activated, cot_low)
    grad_gate = matmul_at(normed_part, d_gate)
    grad_up = matmul_at(normed_part, d_up)
    back_part = matmul_bt(d_gate, gate_all) + matmul_bt(d_up, up_all)
    norm_two_pull = jax.vjp(rms_norm, res_rows, gain_two_f)[1]
    d_normed_two = lax.psum(back_part, "mp")
    d_res_norm, grad_gain_two = norm_two_pull(d_normed_two)
    d_resid = cot_flat + d_res_norm
    mlp_grads = (
        lax.psum_scatter(
            grad_gain_two.astype(jnp.bfloat16), "dp", scatter_dimension=0, tiled=True
        ).astype(jnp.float32),
        lax.psum_scatter(
            grad_gate.astype(jnp.bfloat16), "dp", scatter_dimension=0, tiled=True
        ).astype(jnp.float32),
        lax.psum_scatter(
            grad_up.astype(jnp.bfloat16), "dp", scatter_dimension=0, tiled=True
        ).astype(jnp.float32),
        lax.psum_scatter(
            grad_down.astype(jnp.bfloat16), "dp", scatter_dimension=1, tiled=True
        ).astype(jnp.float32),
    )
    gain_one, query_all, key_all, value_all, beta_all, taps_all, head_all, out_all = (
        lax.all_gather(norm_gain, "dp", axis=0, tiled=True),
        lax.all_gather(w_query, "dp", axis=0, tiled=True),
        lax.all_gather(w_key, "dp", axis=0, tiled=True),
        lax.all_gather(w_value, "dp", axis=0, tiled=True),
        lax.all_gather(w_beta, "dp", axis=0, tiled=True),
        lax.all_gather(conv_taps, "dp", axis=2, tiled=True),
        lax.all_gather(head_gain, "dp", axis=0, tiled=True),
        lax.all_gather(w_out, "dp", axis=1, tiled=True),
    )
    d_att = d_resid.astype(jnp.bfloat16)
    d_head = matmul_bt(d_att, out_all)
    grad_out = matmul_at(head_normed, d_att)
    head_pull = jax.vjp(rms_norm, core_out, head_gain_f)[1]
    d_core, grad_head_part = head_pull(d_head.reshape(core_out.shape))
    dq_rows, dk_rows, dv_rows, db_rows = core_pull(d_core)
    dq_proj, dk_proj, dv_proj, db_logit, grad_taps = mix_pull(
        (rounded(dq_rows), rounded(dk_rows), rounded(dv_rows), db_rows)
    )
    dq_low = dq_proj.reshape(row_total, -1).astype(jnp.bfloat16)
    dk_low = dk_proj.reshape(row_total, -1).astype(jnp.bfloat16)
    dv_low = dv_proj.reshape(row_total, -1).astype(jnp.bfloat16)
    db_low = db_logit.reshape(row_total, -1).astype(jnp.bfloat16)
    grad_query = matmul_at(normed, dq_low)
    grad_key = matmul_at(normed, dk_low)
    grad_value = matmul_at(normed, dv_low)
    grad_beta = matmul_at(normed, db_low)
    d_normed_part = (
        matmul_bt(dq_low, query_all)
        + matmul_bt(dk_low, key_all)
        + matmul_bt(dv_low, value_all)
        + matmul_bt(db_low, beta_all)
    )
    d_normed, grad_head = (
        lax.psum(d_normed_part.astype(jnp.bfloat16), "mp").astype(jnp.float32),
        lax.psum(grad_head_part.astype(jnp.bfloat16), "mp").astype(jnp.float32),
    )
    norm_one_pull = jax.vjp(rms_norm, flat_in, gain_one_f)[1]
    d_in_norm, grad_gain_one = norm_one_pull(d_normed)
    token_grad = (d_resid + d_in_norm).reshape(seq_rows, length, width)
    mixer_grads = (
        lax.psum_scatter(
            grad_gain_one.astype(jnp.bfloat16), "dp", scatter_dimension=0, tiled=True
        ).astype(jnp.float32),
        lax.psum_scatter(
            grad_query.astype(jnp.bfloat16), "dp", scatter_dimension=0, tiled=True
        ).astype(jnp.float32),
        lax.psum_scatter(
            grad_key.astype(jnp.bfloat16), "dp", scatter_dimension=0, tiled=True
        ).astype(jnp.float32),
        lax.psum_scatter(
            grad_value.astype(jnp.bfloat16), "dp", scatter_dimension=0, tiled=True
        ).astype(jnp.float32),
        lax.psum_scatter(
            grad_beta.astype(jnp.bfloat16), "dp", scatter_dimension=0, tiled=True
        ).astype(jnp.float32),
        lax.psum_scatter(
            grad_taps.astype(jnp.bfloat16), "dp", scatter_dimension=2, tiled=True
        ).astype(jnp.float32),
        lax.psum_scatter(
            grad_head.astype(jnp.bfloat16), "dp", scatter_dimension=0, tiled=True
        ).astype(jnp.float32),
        lax.psum_scatter(
            grad_out.astype(jnp.bfloat16), "dp", scatter_dimension=1, tiled=True
        ).astype(jnp.float32),
    )
    return (
        (layer_out.reshape(seq_rows, length, width), token_grad)
        + tuple(mixer_grads)
        + tuple(mlp_grads)
    )


def solution(mesh):
    return jax.shard_map(
        on_device,
        mesh=mesh,
        in_specs=(
            P("dp", None, None),
            P("dp", None),
            P("dp", None, None),
            P("dp"),
            P("dp", "mp"),
            P("dp", "mp"),
            P("dp", "mp"),
            P("dp", "mp"),
            P("mp", None, "dp"),
            P("dp"),
            P("mp", "dp"),
            P("dp"),
            P("dp", "mp"),
            P("dp", "mp"),
            P("mp", "dp"),
        ),
        out_specs=(
            P("dp", None, None),
            P("dp", None, None),
            P("dp"),
            P("dp", "mp"),
            P("dp", "mp"),
            P("dp", "mp"),
            P("dp", "mp"),
            P("mp", None, "dp"),
            P("dp"),
            P("mp", "dp"),
            P("dp"),
            P("dp", "mp"),
            P("dp", "mp"),
            P("mp", "dp"),
        ),
        check_vma=False,
    )
```

profile of v0, /device:TPU:0, one launch (start us, length us, event | category | flops | bytes accessed | tf_op | source)
XLA Modules:
  0.0 1868.0 jit_solution(17711279580496583634)
XLA Ops:
  12.0 22.1 %all-gather = bf16[8,1,128]{2,1,0:T(2,128)(2,1)S(1)} all-gather(bf16[1,1,128]{2,1,0:T(2,128)(2,1)S(1)} %bitcast.874), channel_id=1, replica_groups=mesh['dp'=8,'mp'=4] {'dp'}, dimensions={0}, use_global_device_ids=true | all-gather | bytes 2304 | tf_op jit(solution)/shard_map/all_gather | solution.py:181
  34.1 16.2 all_gather.48
  57.6 31.2 %all_gather.49 = bf16[1024,256]{1,0:T(8,128)(2,1)S(1)} all-gather(bf16[128,256]{1,0:T(8,128)(2,1)S(1)} %copy-done.102), channel_id=1, replica_groups=mesh['dp'=8,'mp'=4] {'dp'}, dimensions={0}, use_global_device_ids=true | all-gather | bytes 589824 | tf_op jit(solution)/shard_map/all_gather | solution.py:184
  93.9 31.4 %all_gather.50 = bf16[1024,256]{1,0:T(8,128)(2,1)S(1)} all-gather(bf16[128,256]{1,0:T(8,128)(2,1)S(1)} %copy-done.103), channel_id=1, replica_groups=mesh['dp'=8,'mp'=4] {'dp'}, dimensions={0}, use_global_device_ids=true | all-gather | bytes 589824 | tf_op jit(solution)/shard_map/all_gather | solution.py:182
  128.8 30.5 %all_gather.47 = bf16[2,12,128]{1,0,2:T(2,128)(2,1)S(1)} all-gather(bf16[2,12,16]{1,0,2:T(2,128)(2,1)S(1)} %copy.537), channel_id=1, replica_groups=mesh['dp'=8,'mp'=4] {'dp'}, dimensions={2}, use_global_device_ids=true | all-gather | bytes 6912 | tf_op jit(solution)/shard_map/all_gather | solution.py:186
  161.3 11.8 fusion.153
  183.8 43.5 %all_gather.46 = bf16[1024,256]{1,0:T(8,128)(2,1)S(1)} all-gather(bf16[128,256]{1,0:T(8,128)(2,1)S(1)} %copy-done.104), channel_id=1, replica_groups=mesh['dp'=8,'mp'=4] {'dp'}, dimensions={0}, use_global_device_ids=true | all-gather | bytes 589824 | tf_op jit(solution)/shard_map/all_gather | solution.py:183
  309.1 229.5 %while.38 = (s32[]{:T(128)}, f32[1,2,128,128]{3,2,1,0:T(8,128)S(1)}, f32[32,1,64,2,128]{4,2,3,1,0:T(8,128)}, f32[32,1,2,128,128]{4,3,2,1,0:T(8,128)}, f32[32,1,6...) while((s32[]{:T(128)}, ...), condition=%wide.region_7.8_spmd.clone, body=%wide.region_6.7_spmd.clone.sunk | while | flops 88358912 | bytes 1774742 | solution.py:133
  547.0 19.2 %all-reduce.35 = bf16[128]{0:T(256)(128)(2,1)S(1)} all-reduce(bf16[128]{0:T(256)(128)(2,1)S(1)} %dynamic-update-slice), channel_id=1, replica_groups=mesh['dp'=8,'mp'=4] {'dp'}, use_global_device_ids=true, to_apply=%add.35 | all-reduce | flops 128 | bytes 512
  566.2 27.2 %all_gather.52 = bf16[256,1024]{1,0:T(8,128)(2,1)S(1)} all-gather(bf16[256,128]{1,0:T(8,128)(2,1)S(1)} %copy-done.105), channel_id=1, replica_groups=mesh['dp'=8,'mp'=4] {'dp'}, dimensions={1}, use_global_device_ids=true | all-gather | bytes 589824 | tf_op jit(solution)/shard_map/all_gather | solution.py:188
  607.2 16.2 all-gather.1
  623.4 132.3 %all-reduce.45.cloned.1.call-done = f32[2048,1024]{1,0:T(8,128)} async-done(((f32[2048,1024]{1,0:T(8,128)}), f32[2048,1024]{1,0:T(8,128)}) %all-reduce.45.cloned.1.call-update) | async-done | bytes 8388624 | tf_op jit(solution)/shard_map/psum | solution.py:227
  767.9 8.3 fusion.245
  776.2 8.4 fusion.246
  784.6 11.9 multiply_convert_fusion.1
  806.1 7.3 convolution_convert_fusion.2
  816.1 7.4 convolution_convert_fusion.1
  841.7 8.0 convolution_convert_fusion
  849.7 109.5 %all-reduce.47.cloned.1.call-done = f32[2048,1024]{1,0:T(8,128)} async-done(((f32[2048,1024]{1,0:T(8,128)}), f32[2048,1024]{1,0:T(8,128)}) %all-reduce.47.cloned.1.call-update) | async-done | bytes 8388624 | tf_op jit(solution)/shard_map/psum | solution.py:263
  959.2 7.6 multiply_reduce_fusion
  994.1 366.2 %while.39 = (s32[]{:T(128)}, f32[1,2,128,128]{2,3,1,0:T(8,128)S(1)}, f32[32,1,64,2,128]{4,2,3,1,0:T(8,128)}, f32[32,1,64,2,128]{4,2,3,1,0:T(8,128)}, f32[32,1,2,...) while((s32[]{:T(128)}, ...), condition=%wide.region_16.17_spmd.clone, body=%wide.region_15.16_spmd.clone.sunk | while | flops 201670656 | bytes 4164839 | solution.py:133
  1360.3 8.4 fusion.85
  1444.5 9.4 multiply_reduce_fusion.7
  1469.6 7.1 multiply_multiply_fusion.2
  1502.7 11.6 add_convert_fusion
  1527.2 49.1 %reduce-scatter.30.cloned.1.call-done = bf16[16,24]{1,0:T(8,128)(2,1)} async-done(((bf16[128,24]{1,0:T(8,128)(2,1)}), bf16[16,24]{1,0:T(8,128)(2,1)}) %reduce-scatter.30.cloned.1.call-update) | async-done | bytes 784
  1577.9 63.1 %reduce-scatter.32.cloned.1.call-done = bf16[128,256]{1,0:T(8,128)(2,1)} async-done(((bf16[1024,256]{1,0:T(8,128)(2,1)}), bf16[128,256]{1,0:T(8,128)(2,1)}) %reduce-scatter.32.cloned.1.call-update) | async-done | bytes 65552
  1642.6 62.8 %reduce-scatter.24.cloned.1.call-done = bf16[128,256]{1,0:T(8,128)(2,1)} async-done(((bf16[1024,256]{1,0:T(8,128)(2,1)}), bf16[128,256]{1,0:T(8,128)(2,1)}) %reduce-scatter.24.cloned.1.call-update) | async-done | bytes 65552 | tf_op jit(solution)/shard_map/reduce_scatter | solution.py:327
  1707.0 63.1 %reduce-scatter.22.cloned.1.call-done = bf16[128,256]{1,0:T(8,128)(2,1)} async-done(((bf16[1024,256]{1,0:T(8,128)(2,1)}), bf16[128,256]{1,0:T(8,128)(2,1)}) %reduce-scatter.22.cloned.1.call-update) | async-done | bytes 65552 | tf_op jit(solution)/shard_map/reduce_scatter | solution.py:324
  1777.3 19.8 %all-reduce.39 = (bf16[1024]{0:T(1024)(128)(2,1)S(1)}, bf16[128]{0:T(256)(128)(2,1)S(1)}, bf16[1024]{0:T(1024)(128)(2,1)S(1)}) all-reduce(bf16[1024]{0:T(1024)(128)(2,1)S(1)} %get-tuple-element.616, bf16[128]{0:T(256)(128)(2,1)S(1)} %bitcast_reduce_fusion, ...), channel_id=2, replica_groups=mesh['dp'=8,'mp'=4] {'dp'}, use_global_device_ids=true, to_apply=%region_24.25.clone | all-reduce | flops 2176 | bytes 8704
  1797.2 37.9 %reduce-scatter.26.cloned.1.call-done = bf16[128,256]{1,0:T(8,128)(2,1)} async-done(((bf16[1024,256]{1,0:T(8,128)(2,1)}), bf16[128,256]{1,0:T(8,128)(2,1)}) %reduce-scatter.26.cloned.1.call-update) | async-done | bytes 65552 | tf_op jit(solution)/shard_map/reduce_scatter | solution.py:330
  1844.0 9.7 fusion.81
  (1424 shorter events, 951.3 us)
Async XLA Ops:
  8.0 747.7 %all-reduce.45.cloned.1.call-start = ((), (), s32[]{:S(2)}) async-start(), calls=%async_computation.9 | async-start | bytes 16777216 | tf_op jit(solution)/shard_map/psum | solution.py:227
  8.1 251.3 %copy-start.79 = (f32[64,64]{0,1:T(8,128)}, f32[64,64]{0,1:T(8,128)S(1)}, u32[]{:S(2)}) copy-start(f32[64,64]{0,1:T(8,128)S(1)} %fusion.209) | copy-start | bytes 49156
  8.1 26.0 %copy-start.138 = (bf16[128,2]{0,1:T(2,128)(2,1)S(1)}, bf16[128,2]{0,1:T(2,128)(2,1)}, u32[]{:S(2)}) copy-start(bf16[128,2]{0,1:T(2,128)(2,1)} %param.26) | copy-start | bytes 1540
  8.1 42.1 %copy-start.1 = (bf16[1,2048,1024]{2,1,0:T(8,128)(2,1)S(1)}, bf16[1,2048,1024]{2,1,0:T(8,128)(2,1)}, u32[]{:S(2)}) copy-start(bf16[1,2048,1024]{2,1,0:T(8,128)(2,1)} %param.19) | copy-start | bytes 12582916
  11.4 818.5 %copy-start.87 = (f32[2048]{0:T(1024)}, f32[2048]{0:T(1024)S(1)}, u32[]{:S(2)}) copy-start(f32[2048]{0:T(1024)S(1)} %fusion.216) | copy-start | bytes 24580
  34.1 17.3 copy-start.97
  54.6 39.3 %copy-start.77 = (f32[2048,2]{0,1:T(2,128)}, f32[2048,2]{0,1:T(2,128)S(1)}, u32[]{:S(2)}) copy-start(f32[2048,2]{0,1:T(2,128)S(1)} %fusion.98) | copy-start | bytes 49156
  56.9 176.2 %copy-start.81 = (f32[2048]{0:T(1024)}, f32[2048]{0:T(1024)S(1)}, u32[]{:S(2)}) copy-start(f32[2048]{0:T(1024)S(1)} %get-tuple-element.753) | copy-start | bytes 24580
  56.9 176.2 %copy-start.83 = (f32[2048]{0:T(1024)}, f32[2048]{0:T(1024)S(1)}, u32[]{:S(2)}) copy-start(f32[2048]{0:T(1024)S(1)} %get-tuple-element.754) | copy-start | bytes 24580
  56.9 176.2 %copy-start.85 = (f32[2048]{0:T(1024)}, f32[2048]{0:T(1024)S(1)}, u32[]{:S(2)}) copy-start(f32[2048]{0:T(1024)S(1)} %get-tuple-element.755) | copy-start | bytes 24580
  88.8 37.3 %copy-start.33 = (bf16[2048,1024]{1,0:T(8,128)(2,1)S(1)}, bf16[2048,1024]{1,0:T(8,128)(2,1)}, u32[]{:S(2)}) copy-start(bf16[2048,1024]{1,0:T(8,128)(2,1)} %copy-done.32) | copy-start | bytes 12582916
  182.3 50.0 %copy-start.93 = (f32[2048,2]{0,1:T(2,128)}, f32[2048,2]{0,1:T(2,128)S(1)}, u32[]{:S(2)}) copy-start(f32[2048,2]{0,1:T(2,128)S(1)} %copy.573) | copy-start | bytes 49156
  249.3 43.8 %copy-start.23 = (bf16[1,2048,2,128]{3,1,2,0:T(8,128)(2,1)}, bf16[1,2048,2,128]{3,1,2,0:T(8,128)(2,1)S(1)}, u32[]{:S(2)}) copy-start(bf16[1,2048,2,128]{3,1,2,0:T(8,128)(2,1)S(1)} %fusion.127) | copy-start | bytes 3145732
  541.1 25.1 %copy-start.105 = (bf16[256,128]{1,0:T(8,128)(2,1)S(1)}, bf16[256,128]{1,0:T(8,128)(2,1)}, u32[]{:S(2)}) copy-start(bf16[256,128]{1,0:T(8,128)(2,1)} %param.29) | copy-start | bytes 196612
  566.2 32.2 %copy-start.49 = (f32[32,1,64,2,128]{4,3,2,0,1:T(2,128)S(1)}, f32[32,1,64,2,128]{4,3,2,0,1:T(2,128)}, u32[]{:S(2)}) copy-start(f32[32,1,64,2,128]{4,3,2,0,1:T(2,128)} %copy.582) | copy-start | bytes 6291460
  605.4 162.4 %all-gather.6.cloned.1.call-start = ((), (), s32[]{:S(2)}) async-start(), calls=%async_computation.10 | async-start | bytes 1622016 | tf_op jit(solution)/shard_map/all_gather | solution.py:230
  606.0 170.2 %all-gather.8.cloned.1.call-start = ((), (), s32[]{:S(2)}) async-start(), calls=%async_computation.11 | async-start | bytes 1622016 | tf_op jit(solution)/shard_map/all_gather | solution.py:231
  606.6 178.0 %all-gather.10.cloned.1.call-start = ((), (), s32[]{:S(2)}) async-start(), calls=%async_computation.12 | async-start | bytes 1622016 | tf_op jit(solution)/shard_map/all_gather | solution.py:232
  607.2 352.0 %all-reduce.47.cloned.1.call-start = ((), (), s32[]{:S(2)}) async-start(), calls=%async_computation.13 | async-start | bytes 16777216 | tf_op jit(solution)/shard_map/psum | solution.py:263
  806.0 714.1 %reduce-scatter.34.cloned.1.call-start = ((), (), s32[]{:S(2)}) async-start(), calls=%async_computation.20 | async-start | bytes 1769472
  816.0 706.0 %reduce-scatter.36.cloned.1.call-start = ((), (), s32[]{:S(2)}) async-start(), calls=%async_computation.21 | async-start | bytes 1769472
  826.1 697.7 %reduce-scatter.38.cloned.1.call-start = ((), (), s32[]{:S(2)}) async-start(), calls=%async_computation.22 | async-start | bytes 1769472
  841.5 684.3 %reduce-scatter.28.cloned.1.call-start = ((), (), s32[]{:S(2)}) async-start(), calls=%async_computation.17 | async-start | bytes 294912
  1458.0 118.3 %reduce-scatter.30.cloned.1.call-start = ((), (), s32[]{:S(2)}) async-start(), calls=%async_computation.18 | async-start | bytes 36864
  1461.5 179.5 %reduce-scatter.32.cloned.1.call-start = ((), (), s32[]{:S(2)}) async-start(), calls=%async_computation.19 | async-start | bytes 589824
  1469.5 236.0 %reduce-scatter.24.cloned.1.call-start = ((), (), s32[]{:S(2)}) async-start(), calls=%async_computation.15 | async-start | bytes 589824 | tf_op jit(solution)/shard_map/reduce_scatter | solution.py:327
  1484.5 285.5 %reduce-scatter.22.cloned.1.call-start = ((), (), s32[]{:S(2)}) async-start(), calls=%async_computation.14 | async-start | bytes 589824 | tf_op jit(solution)/shard_map/reduce_scatter | solution.py:324
  1502.5 269.1 %all-reduce.49.cloned.1.call-start = ((), (), s32[]{:S(2)}) async-start(), calls=%async_computation.23 | async-start | bytes 16777216 | tf_op jit(solution)/shard_map/psum | solution.py:241
  1514.4 320.7 %reduce-scatter.26.cloned.1.call-start = ((), (), s32[]{:S(2)}) async-start(), calls=%async_computation.16 | async-start | bytes 589824 | tf_op jit(solution)/shard_map/reduce_scatter | solution.py:330
  1518.7 252.8 %copy-start.88 = (f32[2048]{0:T(1024)S(1)}, f32[2048]{0:T(1024)}, u32[]{:S(2)}) copy-start(f32[2048]{0:T(1024)} %copy-done.87) | copy-start | bytes 24580
  1518.7 252.8 %copy-start.99 = (f32[8,1,128]{2,1,0:T(1,128)S(1)}, f32[8,1,128]{2,1,0:T(1,128)}, u32[]{:S(2)}) copy-start(f32[8,1,128]{2,1,0:T(1,128)} %copy-done.97) | copy-start | bytes 12292
  1771.6 72.3 %copy-start.101 = (f32[2048]{0:T(1024)S(1)}, f32[2048]{0:T(1024)}, u32[]{:S(2)}) copy-start(f32[2048]{0:T(1024)} %copy-done.100) | copy-start | bytes 24580
  (130 other events, 613.1 us)
Sparse Core Ops, SparseCore 0:
  605.5 150.1 all-reduce.44
  806.1 153.0 all-reduce.46
  1514.5 153.4 all-reduce.48
Sparse Core Ops, SparseCore 1:
  607.9 40.4 all-gather.5
  650.3 41.5 all-gather.7
  693.8 41.4 all-gather.9
  816.1 65.3 reduce-scatter.33
  885.3 63.9 reduce-scatter.35
  952.7 63.7 reduce-scatter.37
  1458.1 61.5 reduce-scatter.27
  1523.5 52.8 reduce-scatter.29
  1579.9 61.1 reduce-scatter.31
  1644.4 61.0 reduce-scatter.23
  1709.0 61.0 reduce-scatter.21
  1774.0 61.0 reduce-scatter.25
where the time goes:
time: 1880 us; the launch traced here: 1870 us
  matrix products  584 us (31%)
  waiting for transfers between devices  520 us (28%)
  local copies, waits for them, and re-layouts  299 us (16%)
  blocking collectives  263 us (14%)
  other arithmetic  176 us (9%)
  between operations  19.6 us (1%)
    squeeze x224, local copies, waits for them, and re-layouts, delta_rule(): lax.scan(jax.checkpoint(group_step), start_state, (query_blocks, key_bloc...  144 us
    psum x1, waiting for transfers between devices, on_device(): res_rows = flat_in + lax.psum(mixer_part, 'mp')  132 us
    unnamed x21, waiting for transfers between devices  114 us
    psum x1, waiting for transfers between devices, on_device(): d_normed_two = lax.psum(back_part, 'mp')  110 us
    dot_general x96, matrix products, group_step(): jnp.einsum('zmu,muj->mzj', query_matrix, running_state_value, precision=h...  103 us
    dot_general x96, matrix products, group_step(): jnp.einsum('sbf,bsx->bfx', incoming_keys * last_doc[:, None, None], fresh...  102 us
    dot_general x96, matrix products, group_step(): jnp.einsum('hij,hjv->hiv', scores, fresh_value_rows, precision=highest_pr...  88.1 us
    reduce_scatter x1, waiting for transfers between devices, on_device(): lax.psum_scatter(grad_query.astype(jnp.bfloat16), 'dp', scatter_dimension...  63.1 us
  transfers between devices with their start and end apart: 15, of which 7 were waited for; matrix products, arithmetic and copies ran while one was open for 34% of the time, Pallas kernels for 0%

commit v1 on v0

v1 whole, which is shorter than its diff:
```python
import functools
import jax
import jax.numpy as jnp
from jax import lax
from jax.experimental import pallas as pl
from jax.experimental.pallas import tpu as pltpu
from jax.sharding import PartitionSpec as P

BF = jnp.bfloat16
F32 = jnp.float32
EPS = 1e-06
STEP = 256
DK = 128
VMEM_LIMIT = 58 * 1024 * 1024
FF_PAD = 768
TAP_ROW = 4
HEAD_ROW = 28
CHUNKS = 2
ORDER = (1, 0)


def nn(a, b):
    return lax.dot_general(a, b, (((1,), (0,)), ((), ())), preferred_element_type=F32)


def nt(a, b):
    return lax.dot_general(a, b, (((1,), (1,)), ((), ())), preferred_element_type=F32)


def tn(a, b):
    return lax.dot_general(a, b, (((0,), (0,)), ((), ())), preferred_element_type=F32)


def hi_lo(x):
    high = x.astype(BF)
    return high, (x - high.astype(F32)).astype(BF)


def iota(shape, dim):
    return lax.broadcasted_iota(jnp.int32, shape, dim)


def sigmoid(x):
    return 1.0 / (1.0 + jnp.exp(-x))


def keep(mask, x):
    return jnp.where(mask, x, 0.0)


def doc_starts(ends_ref, places):
    begin = jnp.zeros_like(places)
    for doc in range(ends_ref.shape[0]):
        end = ends_ref[doc]
        begin = jnp.where(places >= end, end, begin)
    return begin


def doc_masks(ends_ref, base):
    rows = doc_starts(ends_ref, base + iota((STEP, DK), 0))
    cols = doc_starts(ends_ref, base + iota((8, STEP), 1))[0:1]
    last = jnp.int32(0)
    for doc in range(ends_ref.shape[0]):
        end = ends_ref[doc]
        last = jnp.where(base + STEP - 1 >= end, end, last)
    same = jnp.concatenate([rows, rows], axis=1) == cols
    return rows, same, rows < base, rows == last, (last < base).astype(F32)


def wide_masks():
    col = iota((64, STEP), 1)
    return [(col // 64 == b).astype(F32).astype(BF) for b in range(4)]


def spread(x, masks):
    return jnp.concatenate([x * m for m in masks], axis=0)


def wide_product(a_parts, b_parts):
    (ah, al), (bh, bl) = a_parts, b_parts
    both = nn(jnp.concatenate([ah, al], axis=0), bh)
    return both[:64] + both[64:] + nn(ah, bl)


def product(a, b):
    ah, al = hi_lo(a)
    bh, bl = hi_lo(b)
    rows = a.shape[0]
    both = nn(jnp.concatenate([ah, al], axis=0), bh)
    return both[:rows] + both[rows:] + nn(ah, bl)


def inverses(lows):
    masks = wide_masks()
    row = iota((64, STEP), 0)
    col = iota((64, STEP), 1)
    inner = col % 64
    quarter = col // 64
    eye = (row == inner).astype(F32)
    n = range(len(lows))

    def split(xs):
        return [hi_lo(x) for x in xs]

    def spreads(parts):
        return [(spread(h, masks), spread(l, masks)) for h, l in parts]

    def products(a, b):
        return [wide_product(a[i], b[i]) for i in n]

    wide = []
    for low in lows:
        total = keep(quarter == 0, low[0:64])
        for b in range(1, 4):
            total = total + keep(quarter == b, low[64 * b : 64 * b + 64])
        wide.append(total)
    small = [keep(row // 8 == inner // 8, w) for w in wide]
    small_p = split(small)
    power = products(small_p, spreads(small_p))
    power_p = split(power)
    power_s = spreads(power_p)
    third = products(small_p, power_s)
    fourth = products(power_p, power_s)
    first = [eye - small[i] + power[i] - third[i] for i in n]
    more = products(split(first), spreads(split(fourth)))
    inv = [first[i] + more[i] for i in n]
    for size in (8, 16, 32):
        pair = (row // (2 * size) == inner // (2 * size)) & (row // size != inner // size)
        off_p = split([keep(pair, w) for w in wide])
        inv_p = split(inv)
        mid = products(off_p, spreads(inv_p))
        more = products(inv_p, spreads(split(mid)))
        inv = [inv[i] - more[i] for i in n]
    off_p = split([keep(quarter == 0, low[64:128]) + keep(quarter == 2, low[192:256]) for low in lows])
    inv_p = split(inv)
    mid_p = split(products(off_p, spreads(inv_p)))
    blank = jnp.zeros((64, STEP), BF)

    def shifted(x):
        return jnp.concatenate([blank, x * masks[0], blank, x * masks[2]], axis=0)

    more = products(inv_p, [(shifted(h), shifted(l)) for h, l in mid_p])
    top, bottom = [], []
    for i in n:
        t, q = inv[i], more[i]
        top.append(
            jnp.concatenate(
                [keep(quarter == 0, t)[:, :128], (keep(quarter == 1, t) - keep(quarter == 0, q))[:, :128]], axis=0
            )
        )
        bottom.append(
            jnp.concatenate(
                [keep(quarter == 2, t)[:, 128:], (keep(quarter == 3, t) - keep(quarter == 2, q))[:, 128:]], axis=0
            )
        )
    mid = [product(lows[i][128:, :128], top[i]) for i in n]
    corner = [product(bottom[i], mid[i]) for i in n]
    blank = jnp.zeros((128, 128), F32)
    return [
        jnp.concatenate(
            [jnp.concatenate([top[i], blank], axis=1), jnp.concatenate([-corner[i], bottom[i]], axis=1)], axis=0
        )
        for i in n
    ]


def conv_of(buffer_ref, taps_ref, part, reach, base_row):
    branch, head = divmod(part, 2)
    lanes = slice(part * DK, (part + 1) * DK)
    first = TAP_ROW + head * 12 + branch * 4
    total = buffer_ref[base_row : base_row + STEP, lanes] * taps_ref[first + 3 : first + 4, :]
    for behind in range(1, 4):
        moved = buffer_ref[base_row - behind : base_row - behind + STEP, lanes]
        tap = first + 3 - behind
        total = total + keep(reach[behind], moved * taps_ref[tap : tap + 1, :])
    return total


def tn_product(a, b):
    ah, al = hi_lo(a)
    bh, bl = hi_lo(b)
    both = tn(ah, jnp.concatenate([bh, bl], axis=1))
    n = b.shape[1]
    return both[:, :n] + both[:, n:] + tn(al, bh)


def col_sum(x):
    return jnp.sum(x, axis=0, keepdims=True)


def whole(*shape):
    return pl.BlockSpec(shape, lambda *_: (0,) * len(shape))


def sds(shape, kind):
    return jax.ShapeDtypeStruct(shape, kind)


def params():
    return pltpu.CompilerParams(vmem_limit_bytes=VMEM_LIMIT)


def cost(micros, size=0):
    return pl.CostEstimate(flops=int(micros * 8e8), bytes_accessed=int(size), transcendentals=0)


def any_ref():
    return pl.BlockSpec(memory_space=pl.ANY)


def place_shards(own, shards, target, sems, depth):
    copies = []
    for k, shard in enumerate(shards):
        row = pl.multiple_of((own ^ k) * depth, depth)
        copies.append(pltpu.make_async_copy(shard, target.at[pl.ds(row, depth), :], sems.at[k]))
    for copy in copies:
        copy.start()
    for copy in copies:
        copy.wait()


def feature_rows(shards, depth):
    each = DK // shards
    row = iota((depth * shards, DK), 0)
    col = iota((depth * shards, DK), 1)
    inside = row % depth
    return ((inside < each) & ((row // depth) * each + inside == col)).astype(F32).astype(BF)


def mixer_fwd_kernel(*refs, first_row, shards, depth):
    step = pl.program_id(0)
    if shards:
        me_ref, ends_ref, tok_ref = refs[:3]
        shard_refs, refs = refs[3 : 3 + shards], refs[3 + shards :]
        outs, (buffer, state, sems) = refs[:15], refs[15:]
        w_ref, gain_ref, taps_ref, s_out_ref, halo_out_ref = outs[10:]
        outs = outs[:10]
    else:
        me_ref, ends_ref, tok_ref, w_ref, gain_ref, taps_ref, s_in_ref, halo_ref = refs[:8]
        outs, s_out_ref, halo_out_ref, (buffer, state) = refs[8:18], refs[18], refs[19], refs[20:]
    proj_ref, qkv_ref, beta_ref, mixed_ref, normed_ref, inv_ref, wu_ref, r_ref, pm_ref, state_ref = outs
    base = first_row + step * STEP

    @pl.when(step == 0)
    def _():
        if shards:
            place_shards(me_ref[0], shard_refs, w_ref, sems, depth)
            extra = w_ref[:, 768:896]
            pick = (iota((8, DK), 1) == iota((8, DK), 0) + 2).astype(F32).astype(BF)
            gain_ref[...] = nt(pick, extra)
            taps_ref[...] = tn(extra, feature_rows(shards, depth))[:32]
            state[...] = jnp.zeros_like(state)
            buffer[0:8, :] = jnp.zeros((8, 768), F32)
        else:
            state[...] = s_in_ref[...]
            buffer[0:8, :] = halo_ref[...]

    tok = tok_ref[...].astype(F32)
    scale = lax.rsqrt(jnp.mean(tok * tok, axis=-1, keepdims=True) + EPS)
    low_in = (tok * scale * gain_ref[0:1, :]).astype(BF)
    proj = nn(low_in, w_ref[...])
    buffer[8 : 8 + STEP, :] = proj[:, :768]
    proj_ref[...] = proj[:, :768]
    betas = sigmoid(proj[:, 768:896])
    beta_ref[...] = betas
    beta_t = betas.T
    rows, same, carry, in_last, go_on = doc_masks(ends_ref, base)
    behind = base + iota((STEP, DK), 0) - rows
    reach = [None] + [behind >= s for s in (1, 2, 3)]
    parts = []
    for part in range(6):
        pre = conv_of(buffer, taps_ref, part, reach, 8)
        act = pre * sigmoid(pre)
        if part < 4:
            norm = lax.rsqrt(jnp.sum(act * act, axis=-1, keepdims=True) + EPS)
            act = act * norm
            if part < 2:
                act = act * DK**-0.5
        parts.append(act.astype(BF))
    halo_out_ref[...] = buffer[STEP : STEP + 8, :]
    buffer[0:8, :] = buffer[STEP : STEP + 8, :]
    qkv_ref[...] = jnp.concatenate(parts, axis=1)
    at_row = iota((STEP, STEP), 0)
    at_col = iota((STEP, STEP), 1)
    strict = same & (at_row > at_col)
    lower = same & (at_row >= at_col)
    heads = range(2)
    q, k, v = parts[0:2], parts[2:4], parts[4:6]
    lows = [keep(strict, nt(k[h], k[h]) * betas[:, h : h + 1]) for h in heads]
    invs = inverses(lows)
    head_gain = taps_ref[HEAD_ROW : HEAD_ROW + 1, :]
    for h in heads:
        inv_ref[0, h] = invs[h].astype(BF)
        scaled_h, scaled_l = hi_lo(invs[h] * beta_t[h : h + 1, :])
        kv = jnp.concatenate([k[h], v[h]], axis=1)
        solved = nn(scaled_h, kv) + nn(scaled_l, kv)
        wu_ref[0, h] = solved.astype(BF)
        w = keep(carry, solved[:, :DK])
        both_h, both_l = hi_lo(jnp.concatenate([solved[:, DK:], w], axis=1))
        scores = keep(lower, nt(q[h], k[h])).astype(BF)
        inside = nn(scores, both_h)
        k_last = keep(in_last, k[h].astype(F32)).astype(BF)
        outer = tn(k_last, both_h) + tn(k_last, both_l)
        r = (keep(carry, q[h].astype(F32)) - inside[:, DK:]).astype(BF)
        r_ref[0, h] = r
        pm_ref[0, h] = outer[:, DK:]
        now = state[h]
        now_h, now_l = hi_lo(now)
        state_ref[0, h] = now_h
        out = nn(r, jnp.concatenate([now_h, now_l], axis=1))
        mixed = inside[:, :DK] + out[:, :DK] + out[:, DK:]
        state[h] = go_on * now - product(outer[:, DK:], now) + outer[:, :DK]
        lanes = slice(h * DK, (h + 1) * DK)
        mixed_ref[:, lanes] = mixed
        scale = lax.rsqrt(jnp.mean(mixed * mixed, axis=-1, keepdims=True) + EPS)
        normed_ref[:, lanes] = (mixed * scale * head_gain).astype(BF)
    s_out_ref[...] = state[...]


def mixer_fwd(me, ends, tokens, count, first_row, shards=None, w_in=None, small=None, carried=None):
    width = tokens.shape[1]
    steps = count // STEP
    start = first_row // STEP
    rows = lambda n, at=0: pl.BlockSpec((STEP, n), lambda i: (i + at, 0))
    group = lambda *s: pl.BlockSpec((1,) + s, lambda i: (i,) + (0,) * len(s))
    smem = pl.BlockSpec(memory_space=pltpu.SMEM)
    out_specs = [
        rows(768), rows(768), rows(DK), rows(256), rows(256),
        group(2, STEP, STEP), group(2, STEP, STEP), group(2, STEP, DK), group(2, DK, DK), group(2, DK, DK),
    ]
    out_shape = [
        sds((count, 768), F32), sds((count, 768), BF), sds((count, DK), F32), sds((count, 256), F32),
        sds((count, 256), BF), sds((steps, 2, STEP, STEP), BF), sds((steps, 2, STEP, STEP), BF),
        sds((steps, 2, STEP, DK), BF), sds((steps, 2, DK, DK), F32), sds((steps, 2, DK, DK), BF),
    ]
    scratch = [pltpu.VMEM((STEP + 8, 768), F32), pltpu.VMEM((2, DK, DK), F32)]
    if shards:
        args = [me, ends, tokens, *shards]
        in_specs = [smem, smem, rows(width, start)] + [any_ref()] * len(shards)
        out_specs += [whole(width, 896), whole(8, width), whole(32, DK)]
        out_shape += [sds((width, 896), BF), sds((8, width), F32), sds((32, DK), F32)]
        scratch.append(pltpu.SemaphoreType.DMA((len(shards),)))
    else:
        args = [me, ends, tokens, w_in, *small, *carried]
        in_specs = [
            smem, smem, rows(width, start), whole(width, 896), whole(8, width), whole(32, DK),
            whole(2, DK, DK), whole(8, 768),
        ]
    out_specs += [whole(2, DK, DK), whole(8, 768)]
    out_shape += [sds((2, DK, DK), F32), sds((8, 768), F32)]
    return pl.pallas_call(
        functools.partial(
            mixer_fwd_kernel, first_row=first_row, shards=len(shards) if shards else 0,
            depth=shards[0].shape[0] if shards else 0,
        ),
        grid=(steps,),
        in_specs=in_specs,
        out_specs=out_specs,
        out_shape=out_shape,
        scratch_shapes=scratch,
        compiler_params=params(),
        cost_estimate=cost(5 * steps),
    )(*args)


def mixer_bwd_kernel(*refs, first_row, steps, first, last, shards, depth):
    step = pl.program_id(0)
    (
        me_ref, ends_ref, mine_ref, theirs_ref, tok_ref, proj_ref, prev_ref, before_ref, qkv_ref, beta_ref, mixed_ref, normed_ref,
        inv_ref, wu_ref, r_ref, pm_ref, state_ref, w_ref, wo_ref, gain_ref, taps_ref,
    ) = refs[:21]
    refs = refs[21:]
    if not first:
        gw_in, gwo_in, gsmall_in, gnorm_in, ds_in_ref, halo_ref = refs[:6]
        refs = refs[6:]
    dn_mine, dn_theirs = refs[:2]
    refs = refs[2:]
    if last:
        sends, refs = refs[:shards], refs[shards:]
    else:
        out_refs, refs = refs[:6], refs[6:]
    buffer, ahead, dstate, d_att_s, gw_ref, gwo_ref, gsmall_ref, gnorm_ref = refs
    tile = steps - 1 - step
    base = first_row + tile * STEP
    half = tile // (steps // 2)
    core = me_ref[1] & 1

    @pl.when(step == 0)
    def _():
        if first:
            dstate[...] = jnp.zeros_like(dstate)
            ahead[:, 0:8, :] = jnp.zeros((3, 8, 768), F32)
            gw_ref[...] = jnp.zeros_like(gw_ref)
            gwo_ref[...] = jnp.zeros_like(gwo_ref)
            gsmall_ref[...] = jnp.zeros_like(gsmall_ref)
            gnorm_ref[...] = jnp.zeros_like(gnorm_ref)
        else:
            dstate[...] = ds_in_ref[...]
            ahead[:, 0:8, :] = halo_ref[...]
            gw_ref[...] = gw_in[...]
            gwo_ref[...] = gwo_in[...]
            gsmall_ref[...] = gsmall_in[...]
            gnorm_ref[...] = gnorm_in[...]

    @pl.when(half == core)
    def _():
        d_att_s[...] = mine_ref[...]

    @pl.when(half != core)
    def _():
        d_att_s[...] = theirs_ref[...]

    ahead[:, STEP : STEP + 8, :] = ahead[:, 0:8, :]
    d_att = d_att_s[...]
    d_head = nn(d_att, wo_ref[...])
    gwo_ref[...] += tn(d_att, normed_ref[...])
    rows, same, carry, in_last, go_on = doc_masks(ends_ref, base)
    at_row = iota((STEP, STEP), 0)
    at_col = iota((STEP, STEP), 1)
    strict = same & (at_row > at_col)
    lower = same & (at_row >= at_col)
    strict_t = same & (at_row < at_col)
    lower_t = same & (at_row <= at_col)
    betas = beta_ref[...]
    beta_t = betas.T
    heads = range(2)
    d_mixer = [None] * 6
    lane = iota((STEP, DK), 1)
    d_beta = jnp.zeros((STEP, DK), F32)
    head_gain = taps_ref[HEAD_ROW : HEAD_ROW + 1, :]
    for h in heads:
        lanes = slice(h * DK, (h + 1) * DK)
        mixed = mixed_ref[:, lanes]
        e = d_head[:, lanes]
        scale = lax.rsqrt(jnp.mean(mixed * mixed, axis=-1, keepdims=True) + EPS)
        unit = mixed * scale
        gsmall_ref[HEAD_ROW : HEAD_ROW + 1, :] += col_sum(e * unit)
        ge = e * head_gain
        d_out = (scale * (ge - unit * jnp.mean(unit * ge, axis=-1, keepdims=True))).astype(BF)
        q = qkv_ref[:, h * DK : (h + 1) * DK]
        k = qkv_ref[:, 256 + h * DK : 256 + (h + 1) * DK]
        v = qkv_ref[:, 512 + h * DK : 512 + (h + 1) * DK]
        wu = wu_ref[0, h]
        inv = inv_ref[0, h]
        r = r_ref[0, h]
        s_in = state_ref[0, h]
        beta_col = betas[:, h : h + 1]
        beta_row = beta_t[h : h + 1, :]
        dst = dstate[h]
        ds_h = dst.astype(BF)
        dstate[h] = go_on * dst - tn_product(pm_ref[0, h], dst) + tn(r, d_out)
        scores_t = keep(lower_t, nt(k, q)).astype(BF)
        k_last = keep(in_last, k.astype(F32)).astype(BF)
        d_x = nn(scores_t, d_out) + nn(k_last, ds_h)
        carried_w = keep(carry, wu[:, :DK].astype(F32)).astype(BF)
        x = (wu[:, DK:].astype(F32) - nn(carried_w, s_in)).astype(BF)
        d_xb = d_x.astype(BF)
        d_scores = keep(lower, nt(d_out, x)).astype(BF)
        d_scores_t = keep(lower_t, nt(x, d_out)).astype(BF)
        back_s = nt(jnp.concatenate([d_out, d_xb], axis=0), s_in)
        d_q = keep(carry, back_s[:STEP]) + nn(d_scores, k)
        d_k = nn(d_scores_t, q) + keep(in_last, nt(x, ds_h))
        d_w = -keep(carry, back_s[STEP:])
        z = tn(inv, jnp.concatenate([d_w.astype(BF), d_xb], axis=1))
        z_b = z.astype(BF)
        d_a = -keep(strict, nt(z_b, wu))
        d_a_t = -keep(strict_t, nt(wu, z_b))
        gram = nt(k, k)
        kv = jnp.concatenate([k, v], axis=1).astype(F32)
        d_b = jnp.sum(d_a * gram + z * kv, axis=-1, keepdims=True)
        d_g = (d_a * beta_col + d_a_t * beta_row).astype(BF)
        d_k = d_k + nn(d_g, k) + beta_col * z[:, :DK]
        d_v = beta_col * z[:, DK:]
        for place, grad in ((h, d_q), (2 + h, d_k), (4 + h, d_v)):
            d_mixer[place] = grad.astype(BF).astype(F32)
        d_beta = jnp.where(lane == h, d_b * beta_col * (1.0 - beta_col), d_beta)
    buffer[0:8, :] = jnp.where(tile == 0, before_ref[...], prev_ref[...])
    buffer[8 : 8 + STEP, :] = proj_ref[...]
    behind = base + iota((STEP, DK), 0) - rows
    reach = [None] + [behind >= s for s in (1, 2, 3)]
    d_proj = []
    for part in range(6):
        branch, head = divmod(part, 2)
        lanes = slice(part * DK, (part + 1) * DK)
        tap0 = TAP_ROW + head * 12 + branch * 4
        pre = conv_of(buffer, taps_ref, part, reach, 8)
        sig = sigmoid(pre)
        act = pre * sig
        grad = d_mixer[part]
        if part < 4:
            norm = lax.rsqrt(jnp.sum(act * act, axis=-1, keepdims=True) + EPS)
            unit = act * norm
            grad = norm * (grad - unit * jnp.sum(unit * grad, axis=-1, keepdims=True))
            if part < 2:
                grad = grad * DK**-0.5
        grad = grad * sig * (1.0 + pre * (1.0 - sig))
        d_in = grad * taps_ref[tap0 + 3 : tap0 + 4, :]
        gsmall_ref[tap0 + 3 : tap0 + 4, :] += col_sum(grad * buffer[8 : 8 + STEP, lanes])
        for s in (1, 2, 3):
            tap = tap0 + 3 - s
            masked = keep(reach[s], grad)
            gsmall_ref[tap : tap + 1, :] += col_sum(masked * buffer[8 - s : 8 - s + STEP, lanes])
            ahead[s - 1, 0:STEP, lanes] = masked
            d_in = d_in + ahead[s - 1, s : s + STEP, lanes] * taps_ref[tap : tap + 1, :]
        d_proj.append(d_in.astype(BF))
    d_proj.append(d_beta.astype(BF))
    d_proj = jnp.concatenate(d_proj, axis=1)
    tok = tok_ref[...].astype(F32)
    unit = tok * lax.rsqrt(jnp.mean(tok * tok, axis=-1, keepdims=True) + EPS)
    low_in = (unit * gain_ref[0:1, :]).astype(BF)
    gw_ref[...] += tn(low_in, d_proj)
    d_normed = nt(d_proj, w_ref[...])
    gnorm_ref[0:1, :] += col_sum(d_normed * unit)

    @pl.when(half == core)
    def _():
        dn_mine[...] = d_normed.astype(BF)

    @pl.when(half != core)
    def _():
        dn_theirs[...] = d_normed.astype(BF)

    @pl.when(step == steps - 1)
    def _():
        if last:
            small = jnp.concatenate([gsmall_ref[...], jnp.zeros((DK - 32, DK), F32)], axis=0).astype(BF)
            spot = (iota((8, DK), 1) == 2) & (iota((8, DK), 0) == 0)
            extra = nt(feature_rows(shards, depth), small)
            extra = extra + tn(gnorm_ref[...].astype(BF), spot.astype(F32).astype(BF))
            gw_ref[:, 768:896] += extra
            for k in range(shards):
                row = pl.multiple_of((me_ref[0] ^ k) * depth, depth)
                sends[k][:, 0:896] = gw_ref[pl.ds(row, depth), :].astype(BF)
                sends[k][:, 896:1152] = gwo_ref[pl.ds(row, depth), :].astype(BF)
        else:
            for out, value in zip(out_refs, (gw_ref, gwo_ref, gsmall_ref, gnorm_ref, dstate)):
                out[...] = value[...]
            out_refs[5][...] = ahead[:, 0:8, :]


def mixer_bwd(me, ends, mine, theirs, tokens, saved, w_in, wo_own, small, first_row, carried, last, shards):
    proj, qkv, betas, mixed, normed, inv, wu, r, pm, states, prev = saved
    count, width = proj.shape[0], tokens.shape[1]
    steps = count // STEP
    per_half = steps // 2
    start = first_row // STEP
    rows = lambda n, at=0: pl.BlockSpec((STEP, n), lambda i, me: (steps - 1 - i + at, 0))
    group = lambda *s: pl.BlockSpec((1,) + s, lambda i, me: (steps - 1 - i,) + (0,) * len(s))

    def half_rows(flip):
        def place(i, me):
            tile = steps - 1 - i
            half, inside = tile // per_half, tile % per_half
            wanted = (me[1] & 1) ^ flip
            return (jnp.where(half == wanted, inside, jnp.where(half > wanted, per_half - 1, 0)), 0)

        return pl.BlockSpec((STEP, width), place)

    in_specs = [
        pl.BlockSpec(memory_space=pltpu.SMEM), half_rows(0), half_rows(1), rows(width, start), rows(768),
        pl.BlockSpec((8, 768), lambda i, me: (jnp.maximum((steps - 1 - i) * (STEP // 8) - 1, 0), 0)),
        whole(8, 768), rows(768), rows(DK), rows(256), rows(256),
        group(2, STEP, STEP), group(2, STEP, STEP), group(2, STEP, DK), group(2, DK, DK), group(2, DK, DK),
        whole(width, 896), whole(width, 256), whole(8, width), whole(32, DK),
    ]
    args = [
        me, ends, mine, theirs, tokens, proj, proj, prev, qkv, betas, mixed, normed, inv, wu, r, pm, states, w_in, wo_own,
        *small,
    ]
    sums = [(width, 896), (width, 256), (32, DK), (8, width), (2, DK, DK), (3, 8, 768)]
    if carried is not None:
        args += carried
        in_specs += [whole(*s) for s in sums]
    depth = width // shards
    out_specs = [half_rows(0), half_rows(1)]
    out_shape = [sds((count // 2, width), BF)] * 2
    if last:
        out_specs += [whole(depth, 1152)] * shards
        out_shape += [sds((depth, 1152), BF)] * shards
    else:
        out_specs += [whole(*s) for s in sums]
        out_shape += [sds(s, F32) for s in sums]
    return pl.pallas_call(
        functools.partial(
            mixer_bwd_kernel, first_row=first_row, steps=steps, first=carried is None, last=last, shards=shards,
            depth=depth,
        ),
        grid_spec=pltpu.PrefetchScalarGridSpec(
            num_scalar_prefetch=1, grid=(steps,), in_specs=in_specs, out_specs=out_specs,
            scratch_shapes=[
                pltpu.VMEM((STEP + 8, 768), F32), pltpu.VMEM((3, STEP + 8, 768), F32), pltpu.VMEM((2, DK, DK), F32),
                pltpu.VMEM((STEP, width), BF), pltpu.VMEM((width, 896), F32), pltpu.VMEM((width, 256), F32),
                pltpu.VMEM((32, DK), F32), pltpu.VMEM((8, width), F32),
            ],
        ),
        out_shape=out_shape,
        compiler_params=params(),
        cost_estimate=cost(6 * steps),
    )(*args)


def mlp_kernel(*refs, steps, shards, depth, ff):
    step = pl.program_id(0)
    me_ref, tok_ref, cot_ref, gain_ref = refs[:4]
    head_refs, refs = refs[4:8], refs[8:]
    if shards:
        shard_refs, wo_refs, refs = refs[:shards], refs[shards : shards + 4], refs[shards + 4 :]
    else:
        g_ref, u_ref, d_ref, wo_ref = refs[:4]
        refs = refs[4:]
    back_mine, back_theirs, down_mine, down_theirs, res_ref, normed_ref, act_ref, dg_ref, du_ref, ggain_ref = refs[:10]
    refs = refs[10:]
    if shards:
        g_ref, u_ref, d_ref, wo_ref, own_ref, heads, raw, raw_wo, sems, wo_sems = refs
    else:
        (heads,) = refs
    own = me_ref[1]

    @pl.when(step == 0)
    def _():
        ggain_ref[...] = jnp.zeros_like(ggain_ref)
        if shards:
            copies = []
            for m in range(4):
                for k in range(shards):
                    row = pl.multiple_of((me_ref[0] ^ k) * depth, depth)
                    copies.append(
                        pltpu.make_async_copy(
                            wo_refs[m].at[pl.ds(k * depth, depth), :], raw_wo.at[own ^ m, pl.ds(row, depth), :],
                            wo_sems.at[m * shards + k],
                        )
                    )
            for copy in copies:
                copy.start()
            place_shards(me_ref[0], shard_refs, raw, sems, depth)
            inside = iota((256, FF_PAD), 1) < ff
            for at in range(0, raw.shape[0], 256):
                here = slice(at, at + 256)
                g_ref[here, :] = keep(inside, raw[here, 256 : 256 + FF_PAD].astype(F32)).astype(BF)
                from_u = 256 + ff - (256 + ff) % 128
                turned = pltpu.roll(
                    raw[here, from_u : from_u + FF_PAD].astype(F32), FF_PAD - (256 + ff) % 128, axis=1
                )
                u_ref[here, :] = keep(inside, turned).astype(BF)
                from_d = 256 + 2 * ff
                d_ref[here, :] = keep(inside, raw[here, from_d : from_d + FF_PAD].astype(F32)).astype(BF)
            for copy in copies:
                copy.wait()
            wo_ref[...] = raw_wo[...]
            own_ref[...] = raw_wo[own]

    for m in range(4):
        heads[own ^ m] = head_refs[m][...]
    attended = nt(heads[0], wo_ref[0])
    for m in range(1, 4):
        attended = attended + nt(heads[m], wo_ref[m])
    res = tok_ref[...].astype(F32) + attended
    unit = res * lax.rsqrt(jnp.mean(res * res, axis=-1, keepdims=True) + EPS)
    normed = (unit * gain_ref[1:2, :]).astype(BF)
    normed_ref[...] = normed
    gate = nn(normed, g_ref[...])
    up = nn(normed, u_ref[...])
    sig = sigmoid(gate)
    silu = gate * sig
    act = (silu * up).astype(BF)
    act_ref[...] = act
    d_hidden = nn(cot_ref[...], d_ref[...])
    d_gate = (d_hidden * up * sig * (1.0 + gate * (1.0 - sig))).astype(BF)
    d_up = (d_hidden * silu).astype(BF)
    dg_ref[...] = d_gate
    du_ref[...] = d_up
    down = nt(act, d_ref[...]).astype(BF)
    back = nt(d_gate, g_ref[...]) + nt(d_up, u_ref[...])
    ggain_ref[0:1, :] += col_sum(back * unit)

    @pl.when(step < steps // 2)
    def _():
        back_theirs[...] = back.astype(BF)
        down_theirs[...] = down

    @pl.when(step >= steps // 2)
    def _():
        back_mine[...] = back.astype(BF)
        down_mine[...] = down
        res_ref[...] = res


def mlp(me, tokens, cot, small, heads, count, first_row, ff, shards=None, wo=None, weights=None):
    width = tokens.shape[1]
    steps = count // STEP
    per_half = steps // 2
    start = first_row // STEP

    def tile(i, me, at=0):
        half = jnp.where(i >= per_half, me[1] & 1, 1 - (me[1] & 1))
        return at + half * per_half + i % per_half

    rows = lambda n, at=0: pl.BlockSpec((STEP, n), lambda i, me: (tile(i, me, at), 0))
    theirs = pl.BlockSpec((STEP, width), lambda i, me: (jnp.minimum(i, per_half - 1), 0))
    mine = pl.BlockSpec((STEP, width), lambda i, me: (jnp.maximum(i - per_half, 0), 0))
    in_specs = [rows(width, start), rows(width, start), whole(8, width)] + [rows(256)] * 4
    args = [me, tokens, cot, small[0], *heads]
    out_specs = [mine, theirs, mine, theirs, mine, rows(width), rows(FF_PAD), rows(FF_PAD), rows(FF_PAD), whole(8, width)]
    halves = (count // 2, width)
    out_shape = [
        sds(halves, BF), sds(halves, BF), sds(halves, BF), sds(halves, BF), sds(halves, F32), sds((count, width), BF),
        sds((count, FF_PAD), BF), sds((count, FF_PAD), BF), sds((count, FF_PAD), BF), sds((8, width), F32),
    ]
    kept = [(width, FF_PAD)] * 3 + [(4, width, 256)]
    scratch = [pltpu.VMEM((4, STEP, 256), BF)]
    if shards:
        in_specs += [any_ref()] * (len(shards) + 4)
        args += [*shards, *wo]
        out_specs += [whole(*s) for s in kept] + [whole(width, 256)]
        out_shape += [sds(s, BF) for s in kept] + [sds((width, 256), BF)]
        scratch += [
            pltpu.VMEM((width, shards[0].shape[1]), BF), pltpu.VMEM((4, width, 256), BF),
            pltpu.SemaphoreType.DMA((len(shards),)), pltpu.SemaphoreType.DMA((4 * len(shards),)),
        ]
    else:
        in_specs += [whole(*s) for s in kept]
        args += weights
    return pl.pallas_call(
        functools.partial(
            mlp_kernel, steps=steps, shards=len(shards) if shards else 0, depth=shards[0].shape[0] if shards else 0,
            ff=ff,
        ),
        grid_spec=pltpu.PrefetchScalarGridSpec(
            num_scalar_prefetch=1, grid=(steps,), in_specs=in_specs, out_specs=out_specs, scratch_shapes=scratch,
        ),
        out_shape=out_shape,
        compiler_params=params(),
        cost_estimate=cost(3.2 * steps),
    )(*args)


def mlp_grads_kernel(me_ref, *refs, chunks, shards, depth, ff):
    step = pl.program_id(0)
    normed, cot, dg, du, act = (refs[i * chunks : (i + 1) * chunks] for i in range(5))
    gain_ref = refs[5 * chunks]
    sends, packed = refs[5 * chunks + 1 : -1], refs[-1]
    each = 256 // depth

    def over_rows(left, right):
        total = tn(left[0][...], right[0][...])
        for a, b in zip(left[1:], right[1:]):
            total = total + tn(a[...], b[...])
        return total

    g_gate = over_rows(normed, dg)
    g_up = over_rows(normed, du)
    g_down = over_rows(cot, act)
    spot = (iota((8, FF_PAD), 1) == ff) & (iota((8, FF_PAD), 0) == 0)
    g_down = g_down + tn(gain_ref[...].astype(BF), spot.astype(F32).astype(BF))
    cut = ff - ff % 128
    turned = pltpu.roll(g_up, ff % 128, axis=1)
    packed[:, 0:cut] = g_gate[:, 0:cut]
    packed[:, cut : cut + 128] = g_gate[:, cut : cut + 128] + turned[:, 0:128]
    packed[:, cut + 128 : 2 * ff] = turned[:, 128 : 2 * ff - cut]
    packed[:, 2 * ff : 2 * ff + FF_PAD] = g_down
    for i in range(len(sends) // each):

        @pl.when(step == i)
        def _(i=i):
            for t in range(each):
                row = pl.multiple_of((t ^ (me_ref[0] % each)) * depth, depth)
                sends[i * each + t][...] = packed[pl.ds(row, depth), :].astype(BF)


def mlp_grads(me, normed, cot, dg, du, act, gain, shards, ff):
    chunks = len(normed)
    count, width = normed[0].shape
    depth = width // shards
    each = 256 // depth
    block = lambda i, me: (me[0] // each) ^ i
    column = lambda at=0: pl.BlockSpec((count, 256), lambda i, me: (at, block(i, me)))
    wide = 2 * ff + FF_PAD
    return pl.pallas_call(
        functools.partial(mlp_grads_kernel, chunks=chunks, shards=shards, depth=depth, ff=ff),
        grid_spec=pltpu.PrefetchScalarGridSpec(
            num_scalar_prefetch=1,
            grid=(width // 256,),
            in_specs=[column()] * chunks
            + [column(c) for c in range(chunks)]
            + [whole(count, FF_PAD)] * (3 * chunks)
            + [pl.BlockSpec((8, 256), lambda i, me: (0, block(i, me)))],
            out_specs=[whole(depth, wide)] * shards,
            scratch_shapes=[pltpu.VMEM((256, wide), F32)],
        ),
        out_shape=[sds((depth, wide), BF)] * shards,
        compiler_params=params(),
        cost_estimate=cost(12),
    )(me, *normed, *([cot] * chunks), *dg, *du, *act, gain)


def norm_back(e, v, gain):
    scale = lax.rsqrt(jnp.mean(v * v, axis=-1, keepdims=True) + EPS)
    unit = v * scale
    ge = e * gain
    return scale * (ge - unit * jnp.mean(unit * ge, axis=-1, keepdims=True))


def resid_kernel(me_ref, p_ref, q_ref, res_ref, cot_ref, gain_ref, d_resid_ref, d_att_ref):
    e = p_ref[...].astype(F32) + q_ref[...].astype(F32)
    d_resid = cot_ref[...].astype(F32) + norm_back(e, res_ref[...], gain_ref[1:2, :])
    d_resid_ref[...] = d_resid
    d_att_ref[...] = d_resid.astype(BF)


def token_kernel(me_ref, p_ref, q_ref, d_resid_ref, tok_ref, gain_ref, out_ref):
    e = p_ref[...].astype(F32) + q_ref[...].astype(F32)
    out_ref[...] = (d_resid_ref[...] + norm_back(e, tok_ref[...].astype(F32), gain_ref[0:1, :])).astype(BF)


def half_call(kernel, me, arrays, full, gain, first_row, outs):
    count, width = arrays[0].shape
    tiles = count // STEP
    start = first_row // STEP
    rows = pl.BlockSpec((STEP, width), lambda i, me: (i, 0))
    out_shape = [sds((count, width), kind) for kind in outs]
    return pl.pallas_call(
        kernel,
        grid_spec=pltpu.PrefetchScalarGridSpec(
            num_scalar_prefetch=1,
            grid=(tiles,),
            in_specs=[rows] * len(arrays)
            + [pl.BlockSpec((STEP, width), lambda i, me: (start + (me[1] & 1) * tiles + i, 0)), whole(8, width)],
            out_specs=[rows] * len(outs),
        ),
        out_shape=out_shape,
        compiler_params=params(),
        cost_estimate=cost(1.5),
    )(me, *arrays, full, gain)


def swap(x, axis, k):
    return lax.ppermute(x, axis, [(i, i ^ k) for i in range(lax.axis_size(axis))])


def pair_sum(own, other):
    return (own.astype(F32) + other.astype(F32)).astype(BF)


def on_device(
    tokens, doc_lengths, cotangent, norm_gain, w_query, w_key, w_value, w_beta, conv_taps, head_gain, w_out, mlp_gain,
    w_gate, w_up, w_down,
):
    seq_rows, length, width = tokens.shape
    shards = lax.axis_size("dp")
    depth = width // shards
    each = conv_taps.shape[2]
    ff = w_gate.shape[1]
    me = jnp.stack([lax.axis_index("dp"), lax.axis_index("mp")]).astype(jnp.int32)
    ends = jnp.cumsum(doc_lengths[0]).astype(jnp.int32)
    flat = tokens.reshape(length, width)
    cot = cotangent.reshape(length, width)
    tall = lambda x: jnp.pad(x, ((0, depth - x.shape[0]), (0, 0)))
    pack = jnp.concatenate(
        [
            w_query, w_key, w_value, w_beta, norm_gain[:, None], mlp_gain[:, None],
            tall(conv_taps.reshape(24, each).T), tall(head_gain[:, None]), jnp.zeros((depth, 99), BF),
        ],
        axis=1,
    )
    mixer_shards = [pack] + [swap(pack, "dp", k) for k in range(1, shards)]
    pack_two = jnp.concatenate(
        [w_out.T, w_gate, w_up, w_down.T, jnp.zeros((depth, FF_PAD - ff), BF)], axis=1
    )
    count = length // CHUNKS
    fwd, carried, w_in, small = [], None, None, None
    for c in range(CHUNKS):
        if c == 0:
            out = mixer_fwd(me, ends, flat, count, 0, shards=mixer_shards)
            w_in, small = out[10], (out[11], out[12])
            carried = out[13:]
            prev = jnp.zeros((8, 768), F32)
        else:
            out = mixer_fwd(me, ends, flat, count, c * count, w_in=w_in, small=small, carried=carried)
            prev = carried[1]
            carried = out[10:]
        fwd.append(list(out[:10]) + [prev])
    mlp_shards = [pack_two]
    far = [swap(pack_two, "dp", k) for k in range(2, shards, 2)]
    near = [swap(x, "dp", 1) for x in [pack_two] + far]
    mlp_shards = [x for pair in zip([pack_two] + far, near) for x in pair]
    wo_own = jnp.concatenate([x[:, :256] for x in mlp_shards], axis=0)
    wo_y = swap(wo_own, "mp", 2)
    wo = [wo_own, swap(wo_own, "mp", 1), wo_y, swap(wo_y, "mp", 1)]
    heads = []
    for c in range(CHUNKS):
        own = fwd[c][4]
        far_heads = swap(own, "mp", 2)
        heads.append([own, swap(own, "mp", 1), far_heads, swap(far_heads, "mp", 1)])
    order = ORDER
    mid, weights, own_wo = [None] * CHUNKS, None, None
    for c in order:
        if weights is None:
            out = mlp(me, flat, cot, small, heads[c], count, c * count, ff, shards=mlp_shards, wo=wo)
            weights, own_wo = list(out[10:14]), out[14]
        else:
            out = mlp(me, flat, cot, small, heads[c], count, c * count, ff, weights=weights)
        mid[c] = out
    resid = [None] * CHUNKS
    for c in order:
        p = pair_sum(mid[c][0], swap(mid[c][1], "mp", 1))
        q = swap(p, "mp", 2)
        d_resid, d_att = half_call(resid_kernel, me, [p, q, mid[c][4]], cot, small[0], c * count, [F32, BF])
        resid[c] = (d_resid, d_att, swap(d_att, "mp", 1))
    ggain = sum(mid[c][9] for c in range(CHUNKS))
    sends = mlp_grads(
        me, [m[5] for m in mid], cot, [m[7] for m in mid], [m[8] for m in mid], [m[6] for m in mid], ggain, shards, ff
    )
    mlp_sum = sum(swap(sends[k], "dp", k).astype(F32) if k else sends[0].astype(F32) for k in range(shards))
    layer = [None] * CHUNKS
    for c in order:
        p = pair_sum(mid[c][2], swap(mid[c][3], "mp", 1))
        q = swap(p, "mp", 2)
        mine = (mid[c][4] + (p.astype(F32) + q.astype(F32))).astype(BF)
        layer[c] = (mine, swap(mine, "mp", 1))
    carried, token_halves = None, [None] * CHUNKS
    for c in reversed(range(CHUNKS)):
        d_resid, d_att, d_att_other = resid[c]
        out = mixer_bwd(
            me, ends, d_att, d_att_other, flat, fwd[c], w_in, own_wo, small, c * count, carried, c == 0, shards
        )
        carried = list(out[2:])
        p = pair_sum(out[0], swap(out[1], "mp", 1))
        q = swap(p, "mp", 2)
        (mine,) = half_call(token_kernel, me, [p, q, d_resid], flat, small[0], c * count, [BF])
        token_halves[c] = (mine, swap(mine, "mp", 1))
    mix_sum = sum(swap(carried[k], "dp", k).astype(F32) if k else carried[0].astype(F32) for k in range(shards))
    low_core = (me[1] & 1) == 0

    def join(halves):
        parts = []
        for mine, other in halves:
            parts += [jnp.where(low_core, mine, other), jnp.where(low_core, other, mine)]
        return jnp.concatenate(parts, axis=0)

    layer_out = join(layer).reshape(seq_rows, length, width)
    token_grad = join(token_halves).astype(F32).reshape(seq_rows, length, width)
    extra = mix_sum[:, 768:896]
    gains = jnp.concatenate([extra[:, 2], mlp_sum[:, 3 * ff], extra[:each, 28]])
    gains = gains + swap(gains, "mp", 1)
    gains = gains + swap(gains, "mp", 2)
    return (
        layer_out,
        token_grad,
        gains[:depth],
        mix_sum[:, 0:256],
        mix_sum[:, 256:512],
        mix_sum[:, 512:768],
        extra[:, 0:2],
        extra[:each, 4:28].T.reshape(2, 12, each),
        gains[2 * depth :],
        mix_sum[:, 896:1152].T,
        gains[depth : 2 * depth],
        mlp_sum[:, 0:ff],
        mlp_sum[:, ff : 2 * ff],
        mlp_sum[:, 2 * ff : 3 * ff].T,
    )


def solution(mesh):
    return jax.shard_map(
        on_device,
        mesh=mesh,
        in_specs=(
            P("dp", None, None),
            P("dp", None),
            P("dp", None, None),
            P("dp"),
            P("dp", "mp"),
            P("dp", "mp"),
            P("dp", "mp"),
            P("dp", "mp"),
            P("mp", None, "dp"),
            P("dp"),
            P("mp", "dp"),
            P("dp"),
            P("dp", "mp"),
            P("dp", "mp"),
            P("mp", "dp"),
        ),
        out_specs=(
            P("dp", None, None),
            P("dp", None, None),
            P("dp"),
            P("dp", "mp"),
            P("dp", "mp"),
            P("dp", "mp"),
            P("dp", "mp"),
            P("mp", None, "dp"),
            P("dp"),
            P("mp", "dp"),
            P("dp"),
            P("dp", "mp"),
            P("dp", "mp"),
            P("mp", "dp"),
        ),
        check_vma=False,
    )
```

time: 1880 us -> 568 us (0.30)
  matrix products: 584 us -> 0 us
  waiting for transfers between devices: 520 us -> 227 us
  local copies, waits for them, and re-layouts: 299 us -> 28.2 us
  blocking collectives: 263 us -> 0 us
  Pallas kernels: 0 us -> 193 us
  other arithmetic: 176 us -> 26.8 us
  starting transfers between devices: 1.43 us -> 82.1 us
    dot_general x479 -> x0, matrix products: 584 us -> none  [the longest x96 103 us: group_step(): jnp.einsum('zmu,muj->mzj', query_matrix, running_state_value, precision=h...]
    psum x3 -> x0, waiting for transfers between devices: 242 us -> none  [the longest x1 132 us: on_device(): res_rows = flat_in + lax.psum(mixer_part, 'mp')]
    ppermute x0 -> x57, waiting for transfers between devices: none -> 227 us  [swap(): lax.ppermute(x, axis, [(i, i ^ k) for i in range(lax.axis_size(axis))])]
    all_gather x8 -> x0, blocking collectives: 218 us -> none  [the longest x1 43.5 us: on_device(): lax.all_gather(w_key, 'dp', axis=0, tiled=True)]
    pallas_call x0 -> x11, Pallas kernels: none -> 193 us  [the longest x2 57.2 us: mixer_bwd(): pl.pallas_call(functools.partial(mixer_bwd_kernel, first_row=first_row, s...]
    reduce_scatter x3 -> x0, waiting for transfers between devices: 164 us -> none  [the longest x1 63.1 us: on_device(): lax.psum_scatter(grad_query.astype(jnp.bfloat16), 'dp', scatter_dimension...]
    squeeze x224 -> x0, local copies, waits for them, and re-layouts: 144 us -> none  [delta_rule(): lax.scan(jax.checkpoint(group_step), start_state, (query_blocks, key_bloc...]
    unnamed x21 -> x0, waiting for transfers between devices: 114 us -> none
  transfers between devices with their start and end apart: 15 -> 57, of which waited for: 7 -> 20; matrix products, arithmetic and copies ran while one was open for 34% -> 7% of each run, Pallas kernels for 0% -> 35%
where the time goes in v1:
time: 568 us; the launch traced here: 559 us
  waiting for transfers between devices  227 us (40%)
  Pallas kernels  193 us (34%)
  starting transfers between devices  82.1 us (14%)
  local copies, waits for them, and re-layouts  28.2 us (5%)
  other arithmetic  26.8 us (5%)
    ppermute x57, waiting for transfers between devices, swap(): lax.ppermute(x, axis, [(i, i ^ k) for i in range(lax.axis_size(axis))])  227 us
    ppermute x57, starting transfers between devices, swap(): lax.ppermute(x, axis, [(i, i ^ k) for i in range(lax.axis_size(axis))])  82.1 us
    pallas_call x2, Pallas kernels, mixer_bwd(): pl.pallas_call(functools.partial(mixer_bwd_kernel, first_row=first_row, s...  57.2 us
    pallas_call x2, Pallas kernels, mlp(): pl.pallas_call(functools.partial(mlp_kernel, steps=steps, shards=len(shar...  50.2 us
    pallas_call x2, Pallas kernels, mixer_fwd(): pl.pallas_call(functools.partial(mixer_fwd_kernel, first_row=first_row, s...  48 us
    unnamed x125, local copies, waits for them, and re-layouts  20.1 us
    pallas_call x1, Pallas kernels, mlp_grads(): pl.pallas_call(functools.partial(mlp_grads_kernel, chunks=chunks, shards=...  19.2 us
    pallas_call x4, Pallas kernels, half_call(): pl.pallas_call(kernel, grid_spec=pltpu.PrefetchScalarGridSpec(num_scalar_...  18.7 us
  transfers between devices with their start and end apart: 57, of which 20 were waited for; matrix products, arithmetic and copies ran while one was open for 7% of the time, Pallas kernels for 35%

profile of v1, /device:TPU:0, one launch (start us, length us, event | category | flops | bytes accessed | tf_op | source)
XLA Modules:
  0.0 559.5 jit_solution(12078946253714625685)
XLA Ops:
  5.7 6.0 %collective-permute-start.6 = (bf16[128,896]{1,0:T(8,128)(2,1)S(1)}, bf16[128,896]{1,0:T(8,128)(2,1)S(1)}, u32[]{:S(2)}, u32[]{:S(2)}) collective-permute-start(bf16[128,896]{1,0:T(8,128)(2,1)S(1)} %concatenate.33.refs_3_), channel_id=1, source_target_pairs={{0,28},{4,24},{8,20},{12,16},{16,12},{20,8},{24,4},{28,0},{1,29},{... | collective-permute-start | bytes 688136 | tf_op jit(solution)/shard_map/ppermute | solution.py:837
  18.4 21.0 %collective-permute-start.1 = (bf16[128,896]{1,0:T(8,128)(2,1)S(1)}, bf16[128,896]{1,0:T(8,128)(2,1)S(1)}, u32[]{:S(2)}, u32[]{:S(2)}) collective-permute-start(bf16[128,896]{1,0:T(8,128)(2,1)S(1)} %concatenate.33.refs_3_), channel_id=1, source_target_pairs={{0,8},{4,12},{8,0},{12,4},{16,24},{20,28},{24,16},{28,20},{1,9},{5... | collective-permute-start | bytes 688136 | tf_op jit(solution)/shard_map/ppermute | solution.py:837
  50.1 15.8 %collective-permute-done.3.refs_7_ = bf16[128,896]{1,0:T(8,128)(2,1)S(1)} collective-permute-done((bf16[128,896]{1,0:T(8,128)(2,1)S(1)}, bf16[128,896]{1,0:T(8,128)(2,1)S(1)}, u32[]{:S(2)}, u32[]{:S(2)}) %collective-permute-start.3) | collective-permute-done | bytes 229408 | tf_op jit(solution)/shard_map/ppermute | solution.py:837
  68.9 7.2 %collective-permute-start.13 = (bf16[128,2432]{1,0:T(8,128)(2,1)S(1)}, bf16[128,2432]{1,0:T(8,128)(2,1)S(1)}, u32[]{:S(2)}, u32[]{:S(2)}) collective-permute-start(bf16[128,2432]{1,0:T(8,128)(2,1)S(1)} %concatenate.34.refs_8_), channel_id=1, source_target_pairs={{0,4},{4,0},{8,12},{12,8},{16,20},{20,16},{24,28},{28,24},{1,5},{5... | collective-permute-start | bytes 1867784 | tf_op jit(solution)/shard_map/ppermute | solution.py:837
  76.8 24.8 %shard_map.254 = (f32[1024,768]{1,0:T(8,128)}, bf16[1024,768]{1,0:T(8,128)(2,1)}, f32[1024,128]{1,0:T(8,128)}, f32[1024,256]{1,0:T(8,128)}, bf16[1024,256]{1,0:T...) custom-call(s32[2]{0:T(128)} %pad_add_fusion.refs_0_.me_ref, ...), custom_call_target="tpu_custom_call" | custom-call | flops 16000000000 | tf_op jit(solution)/shard_map/pallas_call | solution.py:351
  101.7 23.2 %shard_map.255 = (f32[1024,768]{1,0:T(8,128)}, bf16[1024,768]{1,0:T(8,128)(2,1)}, f32[1024,128]{1,0:T(8,128)}, f32[1024,256]{1,0:T(8,128)}, bf16[1024,256]{1,0:T...) custom-call(s32[2]{0:T(128)} %pad_add_fusion.refs_0_.me_ref, ...), custom_call_target="tpu_custom_call" | custom-call | flops 16000000000 | tf_op jit(solution)/shard_map/pallas_call | solution.py:351
  128.6 18.3 %collective-permute-done.17.refs_13_ = bf16[128,2432]{1,0:T(8,128)(2,1)S(1)} collective-permute-done((bf16[128,2432]{1,0:T(8,128)(2,1)S(1)}, bf16[128,2432]{1,0:T(8,128)(2,1)S(1)}, u32[]{:S(2)}, u32[]{:S(2)}) %collective-permute-start.17) | collective-permute-done | bytes 622624 | tf_op jit(solution)/shard_map/ppermute | solution.py:837
  149.7 7.1 %collective-permute-done.21.refs_18_ = bf16[1024,256]{1,0:T(8,128)(2,1)S(1)} collective-permute-done((bf16[1024,256]{1,0:T(8,128)(2,1)S(1)}, bf16[1024,256]{1,0:T(8,128)(2,1)S(1)}, u32[]{:S(2)}, u32[]{:S(2)}) %collective-permute-start.21) | collective-permute-done | bytes 524320 | tf_op jit(solution)/shard_map/ppermute | solution.py:837
  156.8 5.6 %collective-permute-done.8.refs_6_ = bf16[1024,256]{1,0:T(8,128)(2,1)S(1)} collective-permute-done((bf16[1024,256]{1,0:T(8,128)(2,1)}, bf16[1024,256]{1,0:T(8,128)(2,1)S(1)}, u32[]{:S(2)}, u32[]{:S(2)}) %collective-permute-start.8) | collective-permute-done | bytes 524320 | tf_op jit(solution)/shard_map/ppermute | solution.py:837
  164.7 27.5 %shard_map.256 = (bf16[512,1024]{1,0:T(8,128)(2,1)}, bf16[512,1024]{1,0:T(8,128)(2,1)}, bf16[512,1024]{1,0:T(8,128)(2,1)}, bf16[512,1024]{1,0:T(8,128)(2,1)}, f3...) custom-call(s32[2]{0:T(128)} %pad_add_fusion.refs_0_.me_ref, ...), custom_call_target="tpu_custom_call" | custom-call | flops 10240000000 | tf_op jit(solution)/shard_map/pallas_call | solution.py:723
  192.8 22.7 %shard_map.257 = (bf16[512,1024]{1,0:T(8,128)(2,1)}, bf16[512,1024]{1,0:T(8,128)(2,1)}, bf16[512,1024]{1,0:T(8,128)(2,1)}, bf16[512,1024]{1,0:T(8,128)(2,1)}, f3...) custom-call(s32[2]{0:T(128)} %pad_add_fusion.refs_0_.me_ref, ...), custom_call_target="tpu_custom_call" | custom-call | flops 10240000000 | tf_op jit(solution)/shard_map/pallas_call | solution.py:723
  217.2 19.2 %shard_map.264 = (bf16[128,2176]{1,0:T(8,128)(2,1)}, bf16[128,2176]{1,0:T(8,128)(2,1)}, bf16[128,2176]{1,0:T(8,128)(2,1)}, bf16[128,2176]{1,0:T(8,128)(2,1)}, bf...) custom-call(s32[2]{0:T(128)} %pad_add_fusion.refs_0_.me_ref, ...), custom_call_target="tpu_custom_call" | custom-call | flops 9600000000 | tf_op jit(solution)/shard_map/pallas_call | solution.py:778
  242.7 8.9 %collective-permute-done.48 = bf16[128,2176]{1,0:T(8,128)(2,1)} collective-permute-done((bf16[128,2176]{1,0:T(8,128)(2,1)}, bf16[128,2176]{1,0:T(8,128)(2,1)}, u32[]{:S(2)}, u32[]{:S(2)}) %collective-permute-start.48) | collective-permute-done | bytes 557088 | tf_op jit(solution)/shard_map/ppermute | solution.py:837
  255.2 20.3 %collective-permute-done.50 = bf16[128,2176]{1,0:T(8,128)(2,1)} collective-permute-done((bf16[128,2176]{1,0:T(8,128)(2,1)}, bf16[128,2176]{1,0:T(8,128)(2,1)}, u32[]{:S(2)}, u32[]{:S(2)}) %collective-permute-start.50) | collective-permute-done | bytes 557088 | tf_op jit(solution)/shard_map/ppermute | solution.py:837
  281.6 34.4 %collective-permute-done.51 = bf16[128,2176]{1,0:T(8,128)(2,1)S(1)} collective-permute-done((bf16[128,2176]{1,0:T(8,128)(2,1)}, bf16[128,2176]{1,0:T(8,128)(2,1)S(1)}, u32[]{:S(2)}, u32[]{:S(2)}) %collective-permute-start.51) | collective-permute-done | bytes 557088 | tf_op jit(solution)/shard_map/ppermute | solution.py:837
  316.6 11.1 %collective-permute-done.52 = bf16[128,2176]{1,0:T(8,128)(2,1)S(1)} collective-permute-done((bf16[128,2176]{1,0:T(8,128)(2,1)S(1)}, bf16[128,2176]{1,0:T(8,128)(2,1)S(1)}, u32[]{:S(2)}, u32[]{:S(2)}) %collective-permute-start.52) | collective-permute-done | bytes 557088 | tf_op jit(solution)/shard_map/ppermute | solution.py:837
  333.8 31.1 %collective-permute-done.33.q_ref = bf16[512,1024]{1,0:T(8,128)(2,1)S(1)} collective-permute-done((bf16[512,1024]{1,0:T(8,128)(2,1)S(1)}, bf16[512,1024]{1,0:T(8,128)(2,1)S(1)}, u32[]{:S(2)}, u32[]{:S(2)}) %collective-permute-start.33) | collective-permute-done | bytes 1048608 | tf_op jit(solution)/shard_map/ppermute | solution.py:837
  365.9 4.8 shard_map.259
  377.6 3.2 add_convert_fusion.4
  381.3 6.1 %collective-permute-done.24 = bf16[512,1024]{1,0:T(8,128)(2,1)} collective-permute-done((bf16[512,1024]{1,0:T(8,128)(2,1)}, bf16[512,1024]{1,0:T(8,128)(2,1)}, u32[]{:S(2)}, u32[]{:S(2)}) %collective-permute-start.24) | collective-permute-done | bytes 1048608 | tf_op jit(solution)/shard_map/ppermute | solution.py:837
  389.6 16.4 %collective-permute-done.30.q_ref = bf16[512,1024]{1,0:T(8,128)(2,1)} collective-permute-done((bf16[512,1024]{1,0:T(8,128)(2,1)}, bf16[512,1024]{1,0:T(8,128)(2,1)}, u32[]{:S(2)}, u32[]{:S(2)}) %collective-permute-start.30) | collective-permute-done | bytes 1048608 | tf_op jit(solution)/shard_map/ppermute | solution.py:837
  406.0 4.8 shard_map.258
  410.9 28.1 %shard_map.260 = (bf16[512,1024]{1,0:T(8,128)(2,1)}, bf16[512,1024]{1,0:T(8,128)(2,1)}, f32[1024,896]{1,0:T(8,128)}, f32[1024,256]{1,0:T(8,128)}, f32[32,128]{1,...) custom-call(s32[2]{0:T(128)} %pad_add_fusion.refs_0_.me_ref, s32[8]{0:T(128)} %bitcast.56, ...), custom_call_target="tpu_custom_call" | custom-call | flops 19200000000 | tf_op jit(solution)/shard_map/pallas_call | solution.py:583
  440.1 29.1 %shard_map.261 = (bf16[512,1024]{1,0:T(8,128)(2,1)}, bf16[512,1024]{1,0:T(8,128)(2,1)}, bf16[128,1152]{1,0:T(8,128)(2,1)}, bf16[128,1152]{1,0:T(8,128)(2,1)}, bf...) custom-call(s32[2]{0:T(128)} %pad_add_fusion.refs_0_.me_ref, ...), custom_call_target="tpu_custom_call" | custom-call | flops 19200000000 | tf_op jit(solution)/shard_map/pallas_call | solution.py:583
  481.7 8.0 %collective-permute-done.42 = bf16[128,1152]{1,0:T(8,128)(2,1)S(1)} collective-permute-done((bf16[128,1152]{1,0:T(8,128)(2,1)}, bf16[128,1152]{1,0:T(8,128)(2,1)S(1)}, u32[]{:S(2)}, u32[]{:S(2)}) %collective-permute-start.42) | collective-permute-done | bytes 294944 | tf_op jit(solution)/shard_map/ppermute | solution.py:837
  491.6 4.3 collective-permute-done.43
  500.2 17.4 %collective-permute-done.45 = bf16[128,1152]{1,0:T(8,128)(2,1)S(1)} collective-permute-done((bf16[128,1152]{1,0:T(8,128)(2,1)S(1)}, bf16[128,1152]{1,0:T(8,128)(2,1)S(1)}, u32[]{:S(2)}, u32[]{:S(2)}) %collective-permute-start.45) | collective-permute-done | bytes 294944 | tf_op jit(solution)/shard_map/ppermute | solution.py:837
  518.3 3.7 collective-permute-done.39.q_ref
  523.0 4.5 shard_map.263
  528.0 14.8 %collective-permute-done.36.q_ref = bf16[512,1024]{1,0:T(8,128)(2,1)S(1)} collective-permute-done((bf16[512,1024]{1,0:T(8,128)(2,1)S(1)}, bf16[512,1024]{1,0:T(8,128)(2,1)S(1)}, u32[]{:S(2)}, u32[]{:S(2)}) %collective-permute-start.36) | collective-permute-done | bytes 1048608 | tf_op jit(solution)/shard_map/ppermute | solution.py:837
  543.8 4.5 shard_map.262
  555.1 3.9 maximum_convert_fusion
  (262 shorter events, 99.6 us)
Async XLA Ops:
  12.0 35.8 %collective-permute-start.4 = (bf16[128,896]{1,0:T(8,128)(2,1)S(1)}, bf16[128,896]{1,0:T(8,128)(2,1)S(1)}, u32[]{:S(2)}, u32[]{:S(2)}) collective-permute-start(bf16[128,896]{1,0:T(8,128)(2,1)S(1)} %concatenate.33.refs_3_), channel_id=1, source_target_pairs={{0,20},{4,16},{8,28},{12,24},{16,4},{20,0},{24,12},{28,8},{1,21},{... | collective-permute-start | bytes 688136 | tf_op jit(solution)/shard_map/ppermute | solution.py:837
  12.8 53.1 %collective-permute-start.3 = (bf16[128,896]{1,0:T(8,128)(2,1)S(1)}, bf16[128,896]{1,0:T(8,128)(2,1)S(1)}, u32[]{:S(2)}, u32[]{:S(2)}) collective-permute-start(bf16[128,896]{1,0:T(8,128)(2,1)S(1)} %concatenate.33.refs_3_), channel_id=1, source_target_pairs={{0,16},{4,20},{8,24},{12,28},{16,0},{20,4},{24,8},{28,12},{1,17},{... | collective-permute-start | bytes 688136 | tf_op jit(solution)/shard_map/ppermute | solution.py:837
  14.8 51.1 %collective-permute-start.2 = (bf16[128,896]{1,0:T(8,128)(2,1)S(1)}, bf16[128,896]{1,0:T(8,128)(2,1)S(1)}, u32[]{:S(2)}, u32[]{:S(2)}) collective-permute-start(bf16[128,896]{1,0:T(8,128)(2,1)S(1)} %concatenate.33.refs_3_), channel_id=1, source_target_pairs={{0,12},{4,8},{8,4},{12,0},{16,28},{20,24},{24,20},{28,16},{1,13},{... | collective-permute-start | bytes 688136 | tf_op jit(solution)/shard_map/ppermute | solution.py:837
  18.4 50.5 %collective-permute-start.1 = (bf16[128,896]{1,0:T(8,128)(2,1)S(1)}, bf16[128,896]{1,0:T(8,128)(2,1)S(1)}, u32[]{:S(2)}, u32[]{:S(2)}) collective-permute-start(bf16[128,896]{1,0:T(8,128)(2,1)S(1)} %concatenate.33.refs_3_), channel_id=1, source_target_pairs={{0,8},{4,12},{8,0},{12,4},{16,24},{20,28},{24,16},{28,20},{1,9},{5... | collective-permute-start | bytes 688136 | tf_op jit(solution)/shard_map/ppermute | solution.py:837
  39.4 36.7 %collective-permute-start = (bf16[128,896]{1,0:T(8,128)(2,1)S(1)}, bf16[128,896]{1,0:T(8,128)(2,1)S(1)}, u32[]{:S(2)}, u32[]{:S(2)}) collective-permute-start(bf16[128,896]{1,0:T(8,128)(2,1)S(1)} %concatenate.33.refs_3_), channel_id=1, source_target_pairs={{0,4},{4,0},{8,12},{12,8},{16,20},{20,16},{24,28},{28,24},{1,5},{5... | collective-permute-start | bytes 688136 | tf_op jit(solution)/shard_map/ppermute | solution.py:837
  47.8 78.7 %collective-permute-start.18 = (bf16[128,2432]{1,0:T(8,128)(2,1)S(1)}, bf16[128,2432]{1,0:T(8,128)(2,1)S(1)}, u32[]{:S(2)}, u32[]{:S(2)}) collective-permute-start(bf16[128,2432]{1,0:T(8,128)(2,1)S(1)} %concatenate.34.refs_8_), channel_id=1, source_target_pairs={{0,24},{4,28},{8,16},{12,20},{16,8},{20,12},{24,0},{28,4},{1,25},{... | collective-permute-start | bytes 1867784 | tf_op jit(solution)/shard_map/ppermute | solution.py:837
  65.9 62.5 %collective-permute-start.16 = (bf16[128,2432]{1,0:T(8,128)(2,1)S(1)}, bf16[128,2432]{1,0:T(8,128)(2,1)S(1)}, u32[]{:S(2)}, u32[]{:S(2)}) collective-permute-start(bf16[128,2432]{1,0:T(8,128)(2,1)S(1)} %concatenate.34.refs_8_), channel_id=1, source_target_pairs={{0,16},{4,20},{8,24},{12,28},{16,0},{20,4},{24,8},{28,12},{1,17},{... | collective-permute-start | bytes 1867784 | tf_op jit(solution)/shard_map/ppermute | solution.py:837
  65.9 35.7 %collective-permute-start.14 = (bf16[128,2432]{1,0:T(8,128)(2,1)S(1)}, bf16[128,2432]{1,0:T(8,128)(2,1)S(1)}, u32[]{:S(2)}, u32[]{:S(2)}) collective-permute-start(bf16[128,2432]{1,0:T(8,128)(2,1)S(1)} %concatenate.34.refs_8_), channel_id=1, source_target_pairs={{0,8},{4,12},{8,0},{12,4},{16,24},{20,28},{24,16},{28,20},{1,9},{5... | collective-permute-start | bytes 1867784 | tf_op jit(solution)/shard_map/ppermute | solution.py:837
  68.9 59.6 %collective-permute-start.13 = (bf16[128,2432]{1,0:T(8,128)(2,1)S(1)}, bf16[128,2432]{1,0:T(8,128)(2,1)S(1)}, u32[]{:S(2)}, u32[]{:S(2)}) collective-permute-start(bf16[128,2432]{1,0:T(8,128)(2,1)S(1)} %concatenate.34.refs_8_), channel_id=1, source_target_pairs={{0,4},{4,0},{8,12},{12,8},{16,20},{20,16},{24,28},{28,24},{1,5},{5... | collective-permute-start | bytes 1867784 | tf_op jit(solution)/shard_map/ppermute | solution.py:837
  162.4 30.4 %collective-permute-start.7 = (bf16[1024,256]{1,0:T(8,128)(2,1)}, bf16[1024,256]{1,0:T(8,128)(2,1)}, u32[]{:S(2)}, u32[]{:S(2)}) collective-permute-start(bf16[1024,256]{1,0:T(8,128)(2,1)} %get-tuple-element.95.refs_4_.refs_11_), channel_id=1, source_target_pairs={{0,1},{1,0},{2,3},{3,2},{4,5},{5,4},{6,7},{7,6},{8,9},{9,8},{10,11... | collective-permute-start | bytes 1572872 | tf_op jit(solution)/shard_map/ppermute | solution.py:837
  162.4 30.4 %collective-permute-start.9 = (bf16[1024,256]{1,0:T(8,128)(2,1)S(1)}, bf16[1024,256]{1,0:T(8,128)(2,1)}, u32[]{:S(2)}, u32[]{:S(2)}) collective-permute-start(bf16[1024,256]{1,0:T(8,128)(2,1)S(1)} %collective-permute-done.8.refs_6_), channel_id=1, source_target_pairs={{0,1},{1,0},{2,3},{3,2},{4,5},{5,4},{6,7},{7,6},{8,9},{9,8},{10,11... | collective-permute-start | bytes 1572872 | tf_op jit(solution)/shard_map/ppermute | solution.py:837
  192.2 45.0 %collective-permute-start.26 = (bf16[512,1024]{1,0:T(8,128)(2,1)}, bf16[512,1024]{1,0:T(8,128)(2,1)}, u32[]{:S(2)}, u32[]{:S(2)}) collective-permute-start(bf16[512,1024]{1,0:T(8,128)(2,1)} %get-tuple-element.110), channel_id=1, source_target_pairs={{0,1},{1,0},{2,3},{3,2},{4,5},{5,4},{6,7},{7,6},{8,9},{9,8},{10,11... | collective-permute-start | bytes 3145736 | tf_op jit(solution)/shard_map/ppermute | solution.py:837
  192.5 84.6 %collective-permute-start.32 = (bf16[512,1024]{1,0:T(8,128)(2,1)}, bf16[512,1024]{1,0:T(8,128)(2,1)S(1)}, u32[]{:S(2)}, u32[]{:S(2)}) collective-permute-start(bf16[512,1024]{1,0:T(8,128)(2,1)} %get-tuple-element.125), channel_id=1, source_target_pairs={{0,1},{1,0},{2,3},{3,2},{4,5},{5,4},{6,7},{7,6},{8,9},{9,8},{10,11... | collective-permute-start | bytes 3145736 | tf_op jit(solution)/shard_map/ppermute | solution.py:837
  215.5 62.9 %collective-permute-start.23 = (bf16[512,1024]{1,0:T(8,128)(2,1)}, bf16[512,1024]{1,0:T(8,128)(2,1)}, u32[]{:S(2)}, u32[]{:S(2)}) collective-permute-start(bf16[512,1024]{1,0:T(8,128)(2,1)} %get-tuple-element.107), channel_id=1, source_target_pairs={{0,1},{1,0},{2,3},{3,2},{4,5},{5,4},{6,7},{7,6},{8,9},{9,8},{10,11... | collective-permute-start | bytes 3145736 | tf_op jit(solution)/shard_map/ppermute | solution.py:837
  237.2 38.3 %collective-permute-start.50 = (bf16[128,2176]{1,0:T(8,128)(2,1)}, bf16[128,2176]{1,0:T(8,128)(2,1)}, u32[]{:S(2)}, u32[]{:S(2)}) collective-permute-start(bf16[128,2176]{1,0:T(8,128)(2,1)} %get-tuple-element.169), channel_id=1, source_target_pairs={{0,12},{4,8},{8,4},{12,0},{16,28},{20,24},{24,20},{28,16},{1,13},{... | collective-permute-start | bytes 1671176 | tf_op jit(solution)/shard_map/ppermute | solution.py:837
  251.7 64.4 %collective-permute-start.51 = (bf16[128,2176]{1,0:T(8,128)(2,1)}, bf16[128,2176]{1,0:T(8,128)(2,1)S(1)}, u32[]{:S(2)}, u32[]{:S(2)}) collective-permute-start(bf16[128,2176]{1,0:T(8,128)(2,1)} %get-tuple-element.170), channel_id=1, source_target_pairs={{0,16},{4,20},{8,24},{12,28},{16,0},{20,4},{24,8},{28,12},{1,17},{... | collective-permute-start | bytes 1671176 | tf_op jit(solution)/shard_map/ppermute | solution.py:837
  253.1 74.6 %collective-permute-start.52 = (bf16[128,2176]{1,0:T(8,128)(2,1)S(1)}, bf16[128,2176]{1,0:T(8,128)(2,1)S(1)}, u32[]{:S(2)}, u32[]{:S(2)}) collective-permute-start(bf16[128,2176]{1,0:T(8,128)(2,1)S(1)} %copy-done.32), channel_id=1, source_target_pairs={{0,20},{4,16},{8,28},{12,24},{16,4},{20,0},{24,12},{28,8},{1,21},{... | collective-permute-start | bytes 1671176 | tf_op jit(solution)/shard_map/ppermute | solution.py:837
  275.5 52.7 %collective-permute-start.53 = (bf16[128,2176]{1,0:T(8,128)(2,1)S(1)}, bf16[128,2176]{1,0:T(8,128)(2,1)S(1)}, u32[]{:S(2)}, u32[]{:S(2)}) collective-permute-start(bf16[128,2176]{1,0:T(8,128)(2,1)S(1)} %copy-done.31), channel_id=1, source_target_pairs={{0,24},{4,28},{8,16},{12,20},{16,8},{20,12},{24,0},{28,4},{1,25},{... | collective-permute-start | bytes 1671176 | tf_op jit(solution)/shard_map/ppermute | solution.py:837
  277.0 52.7 %collective-permute-start.54 = (bf16[128,2176]{1,0:T(8,128)(2,1)S(1)}, bf16[128,2176]{1,0:T(8,128)(2,1)S(1)}, u32[]{:S(2)}, u32[]{:S(2)}) collective-permute-start(bf16[128,2176]{1,0:T(8,128)(2,1)S(1)} %copy-done.30), channel_id=1, source_target_pairs={{0,28},{4,24},{8,20},{12,16},{16,12},{20,8},{24,4},{28,0},{1,29},{... | collective-permute-start | bytes 1671176 | tf_op jit(solution)/shard_map/ppermute | solution.py:837
  278.5 53.3 %collective-permute-start.29 = (bf16[512,1024]{1,0:T(8,128)(2,1)S(1)}, bf16[512,1024]{1,0:T(8,128)(2,1)S(1)}, u32[]{:S(2)}, u32[]{:S(2)}) collective-permute-start(bf16[512,1024]{1,0:T(8,128)(2,1)S(1)} %copy-done.29), channel_id=1, source_target_pairs={{0,1},{1,0},{2,3},{3,2},{4,5},{5,4},{6,7},{7,6},{8,9},{9,8},{10,11... | collective-permute-start | bytes 3145736 | tf_op jit(solution)/shard_map/ppermute | solution.py:837
  316.1 61.5 %collective-permute-start.27 = (bf16[512,1024]{1,0:T(8,128)(2,1)}, bf16[512,1024]{1,0:T(8,128)(2,1)}, u32[]{:S(2)}, u32[]{:S(2)}) collective-permute-start(bf16[512,1024]{1,0:T(8,128)(2,1)} %add_convert_fusion.5), channel_id=1, source_target_pairs={{0,2},{1,3},{2,0},{3,1},{4,6},{5,7},{6,4},{7,5},{8,10},{9,11},{10,... | collective-permute-start | bytes 3145736 | tf_op jit(solution)/shard_map/ppermute | solution.py:837
  327.7 37.2 %collective-permute-start.33 = (bf16[512,1024]{1,0:T(8,128)(2,1)S(1)}, bf16[512,1024]{1,0:T(8,128)(2,1)S(1)}, u32[]{:S(2)}, u32[]{:S(2)}) collective-permute-start(bf16[512,1024]{1,0:T(8,128)(2,1)S(1)} %add_convert_fusion.2.p_ref), channel_id=1, source_target_pairs={{0,2},{1,3},{2,0},{3,1},{4,6},{5,7},{6,4},{7,5},{8,10},{9,11},{10,... | collective-permute-start | bytes 3145736 | tf_op jit(solution)/shard_map/ppermute | solution.py:837
  328.2 59.2 %collective-permute-start.24 = (bf16[512,1024]{1,0:T(8,128)(2,1)}, bf16[512,1024]{1,0:T(8,128)(2,1)}, u32[]{:S(2)}, u32[]{:S(2)}) collective-permute-start(bf16[512,1024]{1,0:T(8,128)(2,1)} %add_convert_fusion.7), channel_id=1, source_target_pairs={{0,2},{1,3},{2,0},{3,1},{4,6},{5,7},{6,4},{7,5},{8,10},{9,11},{10,... | collective-permute-start | bytes 3145736 | tf_op jit(solution)/shard_map/ppermute | solution.py:837
  333.3 72.8 %collective-permute-start.30 = (bf16[512,1024]{1,0:T(8,128)(2,1)}, bf16[512,1024]{1,0:T(8,128)(2,1)}, u32[]{:S(2)}, u32[]{:S(2)}) collective-permute-start(bf16[512,1024]{1,0:T(8,128)(2,1)} %add_convert_fusion.3.p_ref), channel_id=1, source_target_pairs={{0,2},{1,3},{2,0},{3,1},{4,6},{5,7},{6,4},{7,5},{8,10},{9,11},{10,... | collective-permute-start | bytes 3145736 | tf_op jit(solution)/shard_map/ppermute | solution.py:837
  370.7 40.2 %collective-permute-start.34 = (bf16[512,1024]{1,0:T(8,128)(2,1)}, bf16[512,1024]{1,0:T(8,128)(2,1)}, u32[]{:S(2)}, u32[]{:S(2)}) collective-permute-start(bf16[512,1024]{1,0:T(8,128)(2,1)} %get-tuple-element.126.refs_2_), channel_id=1, source_target_pairs={{0,1},{1,0},{2,3},{3,2},{4,5},{5,4},{6,7},{7,6},{8,9},{9,8},{10,11... | collective-permute-start | bytes 3145736 | tf_op jit(solution)/shard_map/ppermute | solution.py:837
  380.8 89.7 %collective-permute-start.28 = (bf16[512,1024]{1,0:T(8,128)(2,1)}, bf16[512,1024]{1,0:T(8,128)(2,1)S(1)}, u32[]{:S(2)}, u32[]{:S(2)}) collective-permute-start(bf16[512,1024]{1,0:T(8,128)(2,1)} %add_convert_fusion.4), channel_id=1, source_target_pairs={{0,1},{1,0},{2,3},{3,2},{4,5},{5,4},{6,7},{7,6},{8,9},{9,8},{10,11... | collective-permute-start | bytes 3145736 | tf_op jit(solution)/shard_map/ppermute | solution.py:837
  389.6 82.4 %collective-permute-start.25 = (bf16[512,1024]{1,0:T(8,128)(2,1)S(1)}, bf16[512,1024]{1,0:T(8,128)(2,1)S(1)}, u32[]{:S(2)}, u32[]{:S(2)}) collective-permute-start(bf16[512,1024]{1,0:T(8,128)(2,1)S(1)} %add_convert_fusion.6), channel_id=1, source_target_pairs={{0,1},{1,0},{2,3},{3,2},{4,5},{5,4},{6,7},{7,6},{8,9},{9,8},{10,11... | collective-permute-start | bytes 3145736 | tf_op jit(solution)/shard_map/ppermute | solution.py:837
  410.8 28.6 %collective-permute-start.31 = (bf16[512,1024]{1,0:T(8,128)(2,1)}, bf16[512,1024]{1,0:T(8,128)(2,1)}, u32[]{:S(2)}, u32[]{:S(2)}) collective-permute-start(bf16[512,1024]{1,0:T(8,128)(2,1)} %get-tuple-element.113.refs_2_), channel_id=1, source_target_pairs={{0,1},{1,0},{2,3},{3,2},{4,5},{5,4},{6,7},{7,6},{8,9},{9,8},{10,11... | collective-permute-start | bytes 3145736 | tf_op jit(solution)/shard_map/ppermute | solution.py:837
  438.9 35.8 %collective-permute-start.38 = (bf16[512,1024]{1,0:T(8,128)(2,1)}, bf16[512,1024]{1,0:T(8,128)(2,1)S(1)}, u32[]{:S(2)}, u32[]{:S(2)}) collective-permute-start(bf16[512,1024]{1,0:T(8,128)(2,1)} %get-tuple-element.146), channel_id=1, source_target_pairs={{0,1},{1,0},{2,3},{3,2},{4,5},{5,4},{6,7},{7,6},{8,9},{9,8},{10,11... | collective-permute-start | bytes 3145736 | tf_op jit(solution)/shard_map/ppermute | solution.py:837
  476.5 41.1 %collective-permute-start.45 = (bf16[128,1152]{1,0:T(8,128)(2,1)S(1)}, bf16[128,1152]{1,0:T(8,128)(2,1)S(1)}, u32[]{:S(2)}, u32[]{:S(2)}) collective-permute-start(bf16[128,1152]{1,0:T(8,128)(2,1)S(1)} %copy-done.42), channel_id=1, source_target_pairs={{0,20},{4,16},{8,28},{12,24},{16,4},{20,0},{24,12},{28,8},{1,21},{... | collective-permute-start | bytes 884744 | tf_op jit(solution)/shard_map/ppermute | solution.py:837
  479.2 38.4 %collective-permute-start.46 = (bf16[128,1152]{1,0:T(8,128)(2,1)S(1)}, bf16[128,1152]{1,0:T(8,128)(2,1)S(1)}, u32[]{:S(2)}, u32[]{:S(2)}) collective-permute-start(bf16[128,1152]{1,0:T(8,128)(2,1)S(1)} %copy-done.41), channel_id=1, source_target_pairs={{0,24},{4,28},{8,16},{12,20},{16,8},{20,12},{24,0},{28,4},{1,25},{... | collective-permute-start | bytes 884744 | tf_op jit(solution)/shard_map/ppermute | solution.py:837
  496.2 46.7 %collective-permute-start.36 = (bf16[512,1024]{1,0:T(8,128)(2,1)S(1)}, bf16[512,1024]{1,0:T(8,128)(2,1)S(1)}, u32[]{:S(2)}, u32[]{:S(2)}) collective-permute-start(bf16[512,1024]{1,0:T(8,128)(2,1)S(1)} %add_convert_fusion.1.p_ref), channel_id=1, source_target_pairs={{0,2},{1,3},{2,0},{3,1},{4,6},{5,7},{6,4},{7,5},{8,10},{9,11},{10,... | collective-permute-start | bytes 3145736 | tf_op jit(solution)/shard_map/ppermute | solution.py:837
  (78 other events, 1501.1 us)
